TPU v7x, 128 devices: a whole 4x4x4 slice. The times are simulated.
128 devices in a mesh: section: 8 (over x, core), replica: 4 (over y), dp: 4 (over z).
Axes of the slice: x: 4, y: 4, z: 4, core: 2. Of those that a mesh axis runs over, the one named last changes fastest.
Arguments:
- features: bfloat16 [32, 1024, 512], P(('section', 'dp'), 'replica'), may hold values from -6 to 6
- tile_vals: bfloat16 [32, 4, 8, 48, 128, 128], P(('section', 'dp'), 'replica'), may hold values from -0.078125 to 0.078125
- tile_cols: int32 [32, 4, 8, 48], P(('section', 'dp'), 'replica'), may hold values from 0 to 63, as said below
- row_counts: int32 [32, 4, 8], P(('section', 'dp'), 'replica'), may hold values from 1 to 48, as said below
- degrees: int32 [32, 1024], P(('section', 'dp'), 'replica'), may hold values from 1 to 4
- w_self: bfloat16 [512, 256], replicated, may hold values from -0.25 to 0.25
- w_neigh: bfloat16 [512, 256], replicated, may hold values from -0.25 to 0.25
- cotangent: bfloat16 [32, 1024, 256], P(('section', 'dp'), 'replica'), may hold values from -6 to 6
Outputs:
- hidden: bfloat16 [32, 1024, 256], P(('section', 'dp'), 'replica')
- grad_features: bfloat16 [32, 1024, 512], P(('section', 'dp'), 'replica')
- grad_self: float32 [512, 256], replicated
- grad_neigh: float32 [512, 256], replicated
Inputs may be any that keep to these rules, and one draw needn't show every extreme that they name: `tile_cols`: the 48 column tile numbers of one row tile are distinct. `row_counts`: slots of a row tile from its count on are unused; every device has a row tile with all 48 slots used.
All inputs are finite; a program needn't handle non-finite values.
Results may differ from a plain program's by a relative error of at most 0.022.
Values may be sent and summed in bfloat16 or wider, within the bound.
A program may use at most 128 MiB of HBM per device.

v0:
```python
import math

import jax
import jax.numpy as jnp
from jax import lax
from jax.sharding import PartitionSpec as P


def silu_slope(pre_value):
    sigmoid_v = jax.nn.sigmoid(pre_value)
    return sigmoid_v * (1.0 + pre_value * (1.0 - sigmoid_v))


def build_bands(tile_block, tile_index, col_count):
    selector = (
        tile_index[:, :, None] == jnp.arange(col_count, dtype=jnp.int32)[None, None, :]
    ).astype(tile_block.dtype)
    bands = jnp.einsum("imc,imab->iacb", selector, tile_block, preferred_element_type=jnp.float32)
    edge = tile_block.shape[-1]
    return bands.astype(jnp.bfloat16).reshape(tile_block.shape[0], edge, col_count * edge)


def spread_rows(bands, col_rows):
    spread = jnp.einsum("iak,kf->iaf", bands, col_rows, preferred_element_type=jnp.float32)
    return spread.reshape(-1, col_rows.shape[-1])


def collect_cols(bands, block_grad):
    row_grads = block_grad.reshape(bands.shape[0], bands.shape[1], block_grad.shape[-1])
    return lax.dot_general(
        bands, row_grads, (((0, 1), (0, 1)), ((), ())), preferred_element_type=jnp.float32
    )


def local(features, tile_vals, tile_cols, row_counts, degrees, w_self, w_neigh, cotangent):
    own_rows = features[0]
    row_total = own_rows.shape[0]
    tile_index = tile_cols[0, 0]
    slot_count = tile_index.shape[1]
    slot_live = jnp.arange(slot_count)[None, :] < row_counts[0, 0][:, None]
    tile_block = tile_vals[0, 0] * slot_live[:, :, None, None].astype(tile_vals.dtype)
    edge = tile_block.shape[-1]
    degree_f = degrees[0].astype(jnp.float32)[:, None]
    col_count = lax.axis_size(("section", "dp")) * row_total // edge
    bands = build_bands(tile_block, tile_index, col_count)
    node_scale = 1.0 / math.sqrt(
        row_total * lax.axis_size(("section", "dp")) * lax.axis_size("replica")
    )
    own_cot = cotangent[0].astype(jnp.float32)
    self_term = jnp.dot(own_rows, w_self, preferred_element_type=jnp.float32)
    gathered = lax.all_gather(own_rows, ("section", "dp"), axis=0, tiled=True)
    partial_value = spread_rows(bands, gathered)
    summed = lax.psum_scatter(
        partial_value.astype(jnp.bfloat16), "replica", scatter_dimension=0, tiled=True
    ).astype(jnp.float32)
    aggregate = (summed / degree_f).astype(jnp.bfloat16)
    preact = self_term + jnp.dot(aggregate, w_neigh, preferred_element_type=jnp.float32)
    grad_pre = (own_cot * silu_slope(preact)).astype(jnp.bfloat16)
    grad_agg = (jnp.dot(grad_pre, w_neigh.T, preferred_element_type=jnp.float32) / degree_f).astype(
        jnp.bfloat16
    )
    block_grad = lax.all_gather(grad_agg, "replica", axis=0, tiled=True)
    back_terms = collect_cols(bands, block_grad)
    back_sum = lax.psum_scatter(
        back_terms.astype(jnp.bfloat16), ("section", "dp"), scatter_dimension=0, tiled=True
    ).astype(jnp.float32)
    grad_own = jnp.dot(grad_pre, w_self.T, preferred_element_type=jnp.float32) + back_sum
    neigh_local = jnp.einsum("nd,nf->df", aggregate, grad_pre, preferred_element_type=jnp.float32)
    hidden = jax.nn.silu(preact).astype(jnp.bfloat16)
    self_local = jnp.einsum("nd,nf->df", own_rows, grad_pre, preferred_element_type=jnp.float32)
    grad_self, grad_neigh = lax.psum((self_local, neigh_local), ("section", "replica", "dp"))
    return (
        hidden[None],
        grad_own.astype(jnp.bfloat16)[None],
        grad_self * node_scale,
        grad_neigh * node_scale,
    )


def solution(mesh):
    placed = (
        P(("section", "dp"), "replica", None),
        P(("section", "dp"), "replica", None, None, None, None),
        P(("section", "dp"), "replica", None, None),
        P(("section", "dp"), "replica", None),
        P(("section", "dp"), "replica"),
        P(),
        P(),
        P(("section", "dp"), "replica", None),
    )
    return jax.shard_map(
        local,
        mesh=mesh,
        in_specs=placed,
        out_specs=(
            P(("section", "dp"), "replica", None),
            P(("section", "dp"), "replica", None),
            P(),
            P(),
        ),
        check_vma=False,
    )
```

profile of v0, /device:TPU:1, one launch (start us, length us, event | category | flops | bytes accessed | tf_op | source)
XLA Modules:
  0.0 397.2 jit_solution(18252761666203609787)
XLA Ops:
  7.2 0.0 copy-start
  7.2 0.0 all-gather.6.cloned.1.call-start
  7.2 0.7 all-gather.6.cloned.1.call-update
  7.9 0.0 reduce-scatter.3.cloned.1.call-start
  8.0 0.7 fusion.25
  8.7 0.0 copy-start.4
  8.7 10.7 %bitcast_multiply_fusion = bf16[8,48,128,128]{3,2,1,0:T(8,128)(2,1)} fusion(bf16[1,1,8,48,128,128]{5,4,3,2,1,0:T(8,128)(2,1)} %param.9, bf16[8,48]{1,0:T(8,128)(2,1)S(1)} %fusion.25), kind=kLoop, calls=%fused_computation.4 | loop fusion | flops 6291456 | bytes 25166592 | tf_op jit(solution)/shard_map/mul | solution.py:41
  19.4 0.0 copy-done.4
  19.4 18.8 %fusion.5 = bf16[8,128,128,64]{2,3,1,0:T(8,128)(2,1)} fusion(bf16[8,48,128,128]{3,2,1,0:T(8,128)(2,1)} %bitcast_multiply_fusion, s32[8,48]{1,0:T(8,128)S(1)} %bitcast.54), kind=kOutput, calls=%fused_computation.7 | convolution fusion | flops 813719552 | bytes 29361664 | tf_op jit(solution)/shard_map/imc,imab->iacb/dot_general | solution.py:18
  38.2 28.8 %all-gather.6.cloned.1.call-done = bf16[1,8192,512]{2,1,0:T(8,128)(2,1)} async-done(((bf16[1,256,512]{2,1,0:T(8,128)(2,1)}), bf16[1,8192,512]{2,1,0:T(8,128)(2,1)}) %all-gather.6.cloned.1.call-update) | async-done | bytes 8388624 | tf_op jit(solution)/shard_map/all_gather | solution.py:51
  67.0 0.0 copy-start.5
  67.0 0.0 copy-start.2
  67.0 0.0 copy-start.3
  67.0 0.0 copy-start.7
  67.0 24.6 %fusion.9 = bf16[1024,512]{1,0:T(8,128)(2,1)} fusion(bf16[1,8192,512]{2,1,0:T(8,128)(2,1)} %all-gather.6.cloned.1.call-done, bf16[128,8,64,128]{3,2,1,0:T(8,128)(2,1)} %bitcast.51), kind=kOutput, calls=%fused_computation.9 | convolution fusion | flops 8590458880 | bytes 26214400 | tf_op jit(solution)/shard_map/iak,kf->iaf/dot_general | solution.py:24
  91.6 0.0 reduce-scatter.3.cloned.1.call-update
  91.6 0.0 all-gather.4.cloned.1.call-start
  91.7 0.0 copy-done.5
  91.7 0.0 copy-done.2
  91.7 0.0 copy-done.3
  91.7 0.2 fusion.19
  92.0 21.1 %reduce-scatter.3.cloned.1.call-done = bf16[256,512]{1,0:T(8,128)(2,1)} async-done(((bf16[1024,512]{1,0:T(8,128)(2,1)}), bf16[256,512]{1,0:T(8,128)(2,1)}) %reduce-scatter.3.cloned.1.call-update) | async-done | bytes 262160 | tf_op jit(solution)/shard_map/reduce_scatter | solution.py:53
  113.1 0.0 copy-done
  113.1 0.0 copy-done.7
  113.1 1.9 fusion.17
  115.0 1.0 fusion.15
  116.0 0.0 all-gather.4.cloned.1.call-update
  116.0 0.0 all-reduce.3.cloned.1.call-start
  116.1 0.0 copy-start.6
  116.1 23.4 %copy.20 = bf16[8,128,64,128]{1,3,2,0:T(8,128)(2,1)} copy(bf16[8,128,64,128]{3,2,1,0:T(8,128)(2,1)} %bitcast.52) | data formatting | bytes 33554432 | tf_op jit(solution)/shard_map/reshape | solution.py:20
  139.4 1.0 convolution_bitcast_fusion
  140.5 0.0 copy-done.6
  140.5 1.1 fusion.26
  141.6 0.0 all-reduce.3.cloned.1.call-update
  141.6 0.0 reduce-scatter.5.cloned.1.call-start
  141.7 0.0 all-gather.4.cloned.1.call-done
  141.7 0.0 copy-start.1
  141.7 14.4 %bitcast_convert_fusion = bf16[8192,512]{1,0:T(8,128)(2,1)} fusion(bf16[8,128,8192]{1,2,0:T(8,128)(2,1)} %bitcast.53, bf16[8,128,512]{2,1,0:T(8,128)(2,1)} %bitcast.59), kind=kOutput, calls=%fused_computation.3 | convolution fusion | flops 8594128896 | bytes 26214400 | tf_op jit(solution)/shard_map/dot_general | solution.py:30
  156.1 0.0 reduce-scatter.5.cloned.1.call-update
  156.1 139.3 %all-reduce.3.cloned.1.call-done = (f32[512,256]{0,1:T(8,128)}, f32[512,256]{0,1:T(8,128)}) async-done(((f32[512,256]{0,1:T(8,128)}, f32[512,256]{0,1:T(8,128)}), (f32[512,256]{0,1:T(8,128)}, f32[512,256]{0,1:T(8,128)})) %all-reduce.3.cloned.1.call-update) | async-done | bytes 1048592 | tf_op jit(solution)/shard_map/psum | solution.py:71
  295.4 1.3 broadcast_multiply_fusion
  296.7 1.0 copy.15
  297.7 1.0 copy.16
  298.7 90.0 %reduce-scatter.5.cloned.1.call-done = bf16[256,512]{1,0:T(8,128)(2,1)} async-done(((bf16[8192,512]{1,0:T(8,128)(2,1)}), bf16[256,512]{1,0:T(8,128)(2,1)}) %reduce-scatter.5.cloned.1.call-update) | async-done | bytes 262160 | tf_op jit(solution)/shard_map/reduce_scatter | solution.py:64
  388.8 1.9 fusion.16
  390.7 0.0 copy-done.1
  (1 shorter events, 0.0 us)
Async XLA Ops:
  7.2 105.9 %copy-start = (bf16[512,256]{1,0:T(8,128)(2,1)S(1)}, bf16[512,256]{1,0:T(8,128)(2,1)}, u32[]{:S(2)}) copy-start(bf16[512,256]{1,0:T(8,128)(2,1)} %param.14) | copy-start | bytes 786436
  7.2 59.8 %all-gather.6.cloned.1.call-start = ((), (), s32[]{:S(2)}) async-start(), calls=%async_computation.5 | async-start | bytes 8650752 | tf_op jit(solution)/shard_map/all_gather | solution.py:51
  7.9 105.1 %reduce-scatter.3.cloned.1.call-start = ((), (), s32[]{:S(2)}) async-start(), calls=%async_computation.2 | async-start | bytes 1310720 | tf_op jit(solution)/shard_map/reduce_scatter | solution.py:53
  8.7 10.7 %copy-start.4 = (s32[1,1,8,48]{3,2,1,0:T(8,128)S(1)}, s32[1,1,8,48]{3,2,1,0:T(8,128)}, u32[]{:S(2)}) copy-start(s32[1,1,8,48]{3,2,1,0:T(8,128)} %param.10) | copy-start | bytes 4612
  67.0 24.7 %copy-start.5 = (s32[1,256]{1,0:T(1,128)S(1)}, s32[1,256]{1,0:T(1,128)}, u32[]{:S(2)}) copy-start(s32[1,256]{1,0:T(1,128)} %param.12) | copy-start | bytes 3076
  67.0 24.7 %copy-start.2 = (bf16[1,256,512]{2,1,0:T(8,128)(2,1)S(1)}, bf16[1,256,512]{2,1,0:T(8,128)(2,1)}, u32[]{:S(2)}) copy-start(bf16[1,256,512]{2,1,0:T(8,128)(2,1)} %param.8) | copy-start | bytes 786436
  67.0 24.7 %copy-start.3 = (bf16[512,256]{1,0:T(8,128)(2,1)S(1)}, bf16[512,256]{1,0:T(8,128)(2,1)}, u32[]{:S(2)}) copy-start(bf16[512,256]{1,0:T(8,128)(2,1)} %param.13) | copy-start | bytes 786436
  67.0 46.1 %copy-start.7 = (bf16[1,256,256]{2,1,0:T(8,128)(2,1)S(1)}, bf16[1,256,256]{2,1,0:T(8,128)(2,1)}, u32[]{:S(2)}) copy-start(bf16[1,256,256]{2,1,0:T(8,128)(2,1)} %param.15) | copy-start | bytes 393220
  91.6 50.0 %all-gather.4.cloned.1.call-start = ((), (), s32[]{:S(2)}) async-start(), calls=%async_computation.3 | async-start | bytes 1310720 | tf_op jit(solution)/shard_map/all_gather | solution.py:62
  116.0 179.4 %all-reduce.3.cloned.1.call-start = ((), (), s32[]{:S(2)}) async-start(), calls=%async_computation.6 | async-start | bytes 2097152 | tf_op jit(solution)/shard_map/psum | solution.py:71
  116.1 24.4 %copy-start.6 = (bf16[256,512]{1,0:T(8,128)(2,1)S(1)}, bf16[256,512]{1,0:T(8,128)(2,1)}, u32[]{:S(2)}) copy-start(bf16[256,512]{1,0:T(8,128)(2,1)} %reduce-scatter.3.cloned.1.call-done) | copy-start | bytes 786436
  141.6 247.2 %reduce-scatter.5.cloned.1.call-start = ((), (), s32[]{:S(2)}) async-start(), calls=%async_computation.4 | async-start | bytes 8650752 | tf_op jit(solution)/shard_map/reduce_scatter | solution.py:64
  141.7 249.0 %copy-start.1 = (bf16[512,256]{1,0:T(8,128)(2,1)S(1)}, bf16[512,256]{1,0:T(8,128)(2,1)}, u32[]{:S(2)}) copy-start(bf16[512,256]{1,0:T(8,128)(2,1)} %param.14) | copy-start | bytes 786436
Sparse Core Ops, SparseCore 0:
  10.3 56.6 all-gather.5
  91.8 21.2 reduce-scatter.2
  116.1 24.1 all-gather.3
  146.5 148.8 all-reduce.2
  299.0 89.7 reduce-scatter.4
where the time goes:
time: 399 us; the launch traced here: 397 us
  waiting for transfers between devices  280 us (70%)
  matrix products  65 us (16%)
  local copies, waits for them, and re-layouts  25.4 us (6%)
  between operations  13.9 us (3%)
  other arithmetic  12.8 us (3%)
    psum x1, waiting for transfers between devices, local(): lax.psum((self_local, neigh_local), ('section', 'replica', 'dp'))  139 us
    reduce_scatter x1, waiting for transfers between devices, local(): lax.psum_scatter(back_terms.astype(jnp.bfloat16), ('section', 'dp'), scat...  90 us
    all_gather x1, waiting for transfers between devices, local(): gathered = lax.all_gather(own_rows, ('section', 'dp'), axis=0, tiled=True)  28.8 us
    dot_general x1, matrix products, spread_rows(): jnp.einsum('iak,kf->iaf', bands, col_rows, preferred_element_type=jnp.flo...  24.6 us
    reshape x1, local copies, waits for them, and re-layouts, build_bands(): bands.astype(jnp.bfloat16)  23.4 us
    reduce_scatter x1, waiting for transfers between devices, local(): lax.psum_scatter(partial_value.astype(jnp.bfloat16), 'replica', scatter_d...  21.1 us
    dot_general x1, matrix products, build_bands(): jnp.einsum('imc,imab->iacb', selector, tile_block, preferred_element_type...  18.8 us
    dot_general x1, matrix products, collect_cols(): lax.dot_general(bands, row_grads, (((0, 1), (0, 1)), ((), ())), preferred...  14.4 us
  transfers between devices with their start and end apart: 5, of which 4 were waited for; matrix products, arithmetic and copies ran while one was open for 19% of the time, Pallas kernels for 0%

commit v1 on v0

v1 whole, which is shorter than its diff:
```python
import functools
import math

import jax
import jax.numpy as jnp
from jax import lax
from jax.experimental import pallas as pl
from jax.experimental.pallas import tpu as pltpu
from jax.sharding import PartitionSpec as P

MESH = pl.DeviceIdType.MESH
BF16 = jnp.bfloat16
F32 = jnp.float32
NX = 4
TILE = 128
ROWS = 256
HALF = 128
QUARTER = 64
STRIP = NX * ROWS
N_SEND = 192


def dot(a, b):
    return jnp.dot(a, b, preferred_element_type=F32)


def dot_nt(a, b):
    return lax.dot_general(a, b, (((1,), (1,)), ((), ())), preferred_element_type=F32)


class Links:
    def __init__(self, send_sem, recv_sem):
        self.send_sem, self.recv_sem, self.count, self.sent = send_sem, recv_sem, 0, []

    def send(self, src, dst, device):
        copy = pltpu.make_async_remote_copy(
            src_ref=src,
            dst_ref=dst,
            send_sem=self.send_sem.at[self.count],
            recv_sem=self.recv_sem.at[self.count],
            device_id=device,
            device_id_type=MESH,
        )
        self.count += 1
        copy.start()
        self.sent.append(copy)
        return copy

    def drain(self):
        for copy in self.sent:
            copy.wait_send()


def kernel(
    node_scale,
    x_ref, tiles_hbm, slot_ref, deg_ref, ws_ref, wn_ref, cot_ref,
    hid_ref, gf_ref, gs_ref, gn_ref,
    *scratch,
):
    row_tiles = slot_ref.shape[0]
    tile_refs, scratch = scratch[:row_tiles], scratch[row_tiles:]
    (
        bands, y_all, acc, self_pre, x_t, part_out, part_in, ht, pair_out, pair_in, sums,
        az_s, az_b, bx_s, bx_b, mid_a, mid_b, ax_s, ax_b, bz_s, bz_b, own_gf,
        *rest,
    ) = scratch
    self_bufs, neigh_bufs, (tile_sem, send_sem, recv_sem) = rest[:8], rest[8:16], rest[16:]

    section = lax.axis_index("section")
    x, core = section // 2, section % 2
    y, z = lax.axis_index("replica"), lax.axis_index("dp")
    links = Links(send_sem, recv_sem)

    def at(dx=0, dy=0, dz=0, flip=False):
        c = 1 - core if flip else core
        return {"section": lax.rem(x + dx, NX) * 2 + c, "replica": lax.rem(y + dy, NX), "dp": lax.rem(z + dz, NX)}

    plane = [(dx, dz) for dx in range(NX) for dz in range(NX) if (dx, dz) != (0, 0)]
    barrier = pltpu.get_barrier_semaphore()
    peers = [at(flip=True)] + [at(dy=d) for d in (1, 2, 3)] + [at(dx=dx, dz=dz) for dx, dz in plane]
    for peer in peers:
        pl.semaphore_signal(barrier, inc=1, device_id=peer, device_id_type=MESH)

    tile_copies = []
    slots = tile_refs[0].shape[0] - 1
    for i in range(row_tiles):
        copy = pltpu.make_async_copy(
            tiles_hbm.at[pl.ds(i * slots, slots)], tile_refs[i].at[pl.ds(0, slots)], tile_sem.at[i]
        )
        copy.start()
        tile_copies.append(copy)
        tile_refs[i][slots] = jnp.zeros((TILE, TILE), BF16)

    own = x_ref[...]
    me = (x * 2 + core) * NX + z
    y_all[pl.ds(pl.multiple_of(me * ROWS, ROWS), ROWS), :] = dot(own, wn_ref[...]).astype(BF16)
    pl.semaphore_wait(barrier, len(peers))

    def block(du, dv, h, quarter=None):
        dx, dz = (du, dv) if h == 0 else (dv, du)
        start = ((lax.rem(x + dx, NX) * 2 + core) * NX + lax.rem(z + dz, NX)) * ROWS + h * HALF
        size = HALF
        if quarter is not None:
            start, size = start + quarter * QUARTER, QUARTER
        return y_all.at[pl.ds(pl.multiple_of(start, QUARTER), size), :]

    def step(h, first, d):
        along_x = (h == 0) == first
        return at(dx=d) if along_x else at(dz=d)

    def push(h, first, d, du, dv, quarter=None):
        ref = block(du, dv, h, quarter)
        return links.send(ref, ref, step(h, first, d))

    def to_partner(h, du, dv):
        ref = block(du, dv, h)
        partner[h, du, dv] = links.send(ref, ref, at(flip=True))

    def make_rows(i):
        tile_copies[i].wait()

        def put(q, carry):
            for k in range(4):
                c = q * 4 + k
                bands[pl.ds(i * TILE, TILE), pl.ds(pl.multiple_of(c * TILE, TILE), TILE)] = tile_refs[i][slot_ref[i, c]]
            return carry

        lax.fori_loop(0, slot_ref.shape[1] // 4, put, 0)

    partner, p1, p1q, p2, p2q = {}, {}, {}, {}, {}
    for h in (0, 1):
        p1[h, 3] = push(h, True, 1, 0, 0)
        p1[h, 1] = push(h, True, 3, 0, 0)
    for h in (0, 1):
        p2[h, 0, 3] = push(h, False, 1, 0, 0)
        p2[h, 0, 1] = push(h, False, 3, 0, 0)
    for h in (0, 1):
        to_partner(h, 0, 0)

    self_pre[...] = dot(own, ws_ref[...])
    x_t[...] = own.T
    for i in range(0, 4):
        make_rows(i)

    for h in (0, 1):
        for du in (3, 1):
            p1[h, du].wait_recv()
            back = 1 if du == 3 else 3
            p1q[h, du] = push(h, True, back, du, 0, 0 if du == 3 else 1)
    for du in (3, 1):
        for h in (0, 1):
            p2[h, du, 3] = push(h, False, 1, du, 0)
            p2[h, du, 1] = push(h, False, 3, du, 0)
            to_partner(h, du, 0)
    for i in range(4, 6):
        make_rows(i)

    def relay(du):
        for h in (0, 1):
            for dv in (3, 1):
                p2[h, du, dv].wait_recv()
                p2q[h, du, dv] = push(h, False, 1 if dv == 3 else 3, du, dv, 0 if dv == 3 else 1)
                to_partner(h, du, dv)

    def finish(du):
        for h in (0, 1):
            p2q[h, du, 3].wait_recv()
            p2q[h, du, 1].wait_recv()
            to_partner(h, du, 2)

    relay(0)
    for h in (0, 1):
        p1q[h, 3].wait_recv()
        p1q[h, 1].wait_recv()
        p2[h, 2, 3] = push(h, False, 1, 2, 0)
        p2[h, 2, 1] = push(h, False, 3, 2, 0)
        to_partner(h, 2, 0)
    for i in range(6, 8):
        make_rows(i)

    def strip_of(dx, flip):
        c = 1 - core if flip else core
        return pl.ds(pl.multiple_of((lax.rem(x + dx, NX) * 2 + c) * STRIP, STRIP), STRIP)

    def spread(dx, flip, first=False):
        cols = strip_of(dx, flip)
        value = dot(bands[:, cols], y_all[cols, :])
        acc[...] = value if first else acc[...] + value

    def wait_partner(dx):
        for dz in range(NX):
            partner[0, dx, dz].wait_recv()
            partner[1, dz, dx].wait_recv()

    finish(0)
    relay(3)
    relay(1)
    finish(3)
    finish(1)
    wait_partner(0)
    spread(0, False, True)
    relay(2)
    spread(0, True)
    wait_partner(3)
    spread(3, False)
    spread(3, True)
    finish(2)
    wait_partner(1)
    spread(1, False)
    spread(1, True)
    wait_partner(2)
    own_cols, flip_cols = strip_of(2, False), strip_of(2, True)

    def last_rows(dy):
        rows = pl.ds(pl.multiple_of(lax.rem(y + dy, NX) * ROWS, ROWS), ROWS)
        return acc[rows, :] + dot(bands[rows, own_cols], y_all[own_cols, :]) + dot(bands[rows, flip_cols], y_all[flip_cols, :])

    parts = []
    for d in (2, 1, 3):
        part_out[d - 1] = last_rows(d).astype(BF16)
        parts.append(links.send(part_out.at[d - 1], part_in.at[d - 1], at(dy=d)))
    total = last_rows(0)
    deg = jnp.broadcast_to(deg_ref[...].astype(F32), (ROWS, ROWS)).T
    for part in parts:
        part.wait_recv()
    total = total + part_in[0].astype(F32) + part_in[1].astype(F32) + part_in[2].astype(F32)

    preact = self_pre[...] + total / deg
    sig = jax.nn.sigmoid(preact)
    grad_pre = (cot_ref[...].astype(F32) * (sig * (1.0 + preact * (1.0 - sig)))).astype(BF16)
    scaled = grad_pre.astype(F32) / deg
    own_rows = pl.ds(pl.multiple_of(y * ROWS, ROWS), ROWS)
    ht[:, own_rows] = scaled.T.astype(BF16)
    grads = [links.send(ht.at[:, own_rows], ht.at[:, own_rows], at(dy=d)) for d in (2, 1, 3)]
    hid_ref[...] = (preact * sig).astype(BF16)
    own_gf[...] = dot_nt(grad_pre, ws_ref[...])
    gself = dot(x_t[...], grad_pre)

    def all_sum(value, out_ref, bufs):
        a_out, a_in, b_out, b_in, c_out, c_in, c_all, result = bufs
        depth = a_in.shape[0]
        seg = depth // NX
        mine = pl.ds(pl.multiple_of(core * depth, depth), depth)
        other = pl.ds(pl.multiple_of((1 - core) * depth, depth), depth)
        a_out[...] = value.astype(BF16)
        copy = links.send(a_out.at[other, :], a_in, at(flip=True))
        yield
        copy.wait_recv()
        b_out[...] = (a_out[mine, :].astype(F32) + a_in[...].astype(F32)).astype(BF16)

        def seg_at(d, base=0):
            return pl.ds(pl.multiple_of(base + lax.rem(y + d, NX) * seg, seg), seg)

        copies = [links.send(b_out.at[seg_at(d), :], b_in.at[d - 1], at(dy=d)) for d in (2, 1, 3)]
        yield
        for copy in copies:
            copy.wait_recv()
        c_out[...] = b_out[seg_at(0), :].astype(F32) + b_in[0].astype(F32) + b_in[1].astype(F32) + b_in[2].astype(F32)

        def piece(dx, dz):
            j = lax.rem(x + dx, NX) * NX + lax.rem(z + dz, NX)
            return pl.ds(pl.multiple_of((j // 2) * 8, 8), 8), pl.ds(pl.multiple_of((j % 2) * 128, 128), 128)

        copies = [
            links.send(c_out.at[piece(dx, dz)], c_in.at[n], at(dx=dx, dz=dz)) for n, (dx, dz) in enumerate(plane)
        ]
        yield
        mine_piece = c_out[piece(0, 0)]
        for n, copy in enumerate(copies):
            copy.wait_recv()
            mine_piece = mine_piece + c_in[n]
        c_all[piece(0, 0)] = mine_piece
        copies = [links.send(c_all.at[piece(0, 0)], c_all.at[piece(0, 0)], at(dx=dx, dz=dz)) for dx, dz in plane]
        yield
        for copy in copies:
            copy.wait_recv()
        rows = seg_at(0, core * depth)
        result[rows, :] = c_all[...].astype(BF16)
        copies = [links.send(result.at[rows, :], result.at[rows, :], at(dy=d)) for d in (2, 1, 3)]
        yield
        for copy in copies:
            copy.wait_recv()
        copy = links.send(result.at[mine, :], result.at[mine, :], at(flip=True))
        yield
        copy.wait_recv()
        out_ref[...] = result[...].astype(F32) * node_scale
        yield

    self_sum = all_sum(gself, gs_ref, self_bufs)
    next(self_sum)
    for copy in grads:
        copy.wait_recv()

    def collect(dx, flip):
        return dot(ht[...], bands[:, strip_of(dx, flip)])

    def add(a, b):
        return (a.astype(F32) + b.astype(F32)).astype(BF16)

    pair, a1, a2 = {}, {}, {}
    lo, hi, half_a, half_b = pl.ds(0, QUARTER), pl.ds(QUARTER, QUARTER), pl.ds(0, HALF), pl.ds(HALF, HALF)
    b_lo, b_hi = pl.ds(HALF, QUARTER), pl.ds(HALF + QUARTER, QUARTER)

    def z_at(d):
        return lax.rem(z + d, NX)

    def give(dx):
        value = collect(dx, True).astype(BF16)
        for k in range(NX):
            pair_out[dx, k] = value[:, k * ROWS : (k + 1) * ROWS]
        pair[dx] = links.send(pair_out.at[dx], pair_in.at[dx], at(flip=True))

    def keep(dx):
        value = collect(dx, False)
        pair[dx].wait_recv()
        for k in range(NX):
            sums[dx, k] = (value[:, k * ROWS : (k + 1) * ROWS] + pair_in[dx, k].astype(F32)).astype(BF16)
        a1[dx] = (
            links.send(sums.at[dx, z_at(2), lo], az_s.at[0, dx], at(dz=1)),
            links.send(sums.at[dx, z_at(2), hi], az_s.at[1, dx], at(dz=3)),
        )

    def a_relay(dx):
        up, down = a1[dx]
        up.wait_recv()
        sums[dx, z_at(1), lo] = add(sums[dx, z_at(1), lo], az_s[0, dx])
        first = links.send(sums.at[dx, z_at(1), half_a], az_b.at[0, dx], at(dz=1))
        down.wait_recv()
        sums[dx, z_at(3), hi] = add(sums[dx, z_at(3), hi], az_s[1, dx])
        second = links.send(sums.at[dx, z_at(3), half_a], az_b.at[1, dx], at(dz=3))
        a2[dx] = (first, second)

    def a_close(dx):
        for copy in a2[dx]:
            copy.wait_recv()
        total = sums[dx, z, half_a].astype(F32) + az_b[0, dx].astype(F32) + az_b[1, dx].astype(F32)
        mid_a[dx] = total.astype(BF16)

    give(2)
    give(1)
    keep(2)
    b_up = links.send(sums.at[2, :, b_lo], bx_s.at[0], at(dx=1))
    b_down = links.send(sums.at[2, :, b_hi], bx_s.at[1], at(dx=3))
    give(3)
    next(self_sum)
    keep(1)
    b_up.wait_recv()
    for k in range(NX):
        sums[1, k, b_lo] = add(sums[1, k, b_lo], bx_s[0, k])
    b_up = links.send(sums.at[1, :, half_b], bx_b.at[0], at(dx=1))
    give(0)
    a_relay(2)
    keep(3)
    b_down.wait_recv()
    for k in range(NX):
        sums[3, k, b_hi] = add(sums[3, k, b_hi], bx_s[1, k])
    b_down = links.send(sums.at[3, :, half_b], bx_b.at[1], at(dx=3))
    a_relay(1)
    keep(0)
    a_relay(3)
    a_relay(0)
    next(self_sum)

    a_close(2)
    qa_up = links.send(mid_a.at[2, lo], ax_s.at[0], at(dx=1))
    qa_down = links.send(mid_a.at[2, hi], ax_s.at[1], at(dx=3))
    next(self_sum)
    b_up.wait_recv()
    b_down.wait_recv()
    for k in range(NX):
        total = sums[0, k, half_b].astype(F32) + bx_b[0, k].astype(F32) + bx_b[1, k].astype(F32)
        mid_b[k] = total.astype(BF16)
    qb_up = links.send(mid_b.at[z_at(2), lo], bz_s.at[0], at(dz=1))
    qb_down = links.send(mid_b.at[z_at(2), hi], bz_s.at[1], at(dz=3))
    a_close(1)
    qa_up.wait_recv()
    mid_a[1, lo] = add(mid_a[1, lo], ax_s[0])
    qa_up = links.send(mid_a.at[1], ax_b.at[0], at(dx=1))
    a_close(3)
    qa_down.wait_recv()
    mid_a[3, hi] = add(mid_a[3, hi], ax_s[1])
    qa_down = links.send(mid_a.at[3], ax_b.at[1], at(dx=3))
    next(self_sum)
    qb_up.wait_recv()
    mid_b[z_at(1), lo] = add(mid_b[z_at(1), lo], bz_s[0])
    qb_up = links.send(mid_b.at[z_at(1)], bz_b.at[0], at(dz=1))
    qb_down.wait_recv()
    mid_b[z_at(3), hi] = add(mid_b[z_at(3), hi], bz_s[1])
    qb_down = links.send(mid_b.at[z_at(3)], bz_b.at[1], at(dz=3))
    a_close(0)
    next(self_sum)
    for copy in (qa_up, qa_down, qb_up, qb_down):
        copy.wait_recv()
    sum_a = mid_a[0].astype(F32) + ax_b[0].astype(F32) + ax_b[1].astype(F32)
    sum_b = mid_b[z].astype(F32) + bz_b[0].astype(F32) + bz_b[1].astype(F32)
    back = jnp.concatenate([sum_a, sum_b], axis=0).T.astype(BF16)

    neigh_sum = all_sum(dot(x_t[...], back), gn_ref, neigh_bufs)
    next(neigh_sum)
    gf_ref[...] = (own_gf[...] + dot_nt(back, wn_ref[...])).astype(BF16)
    for _ in self_sum:
        pass
    for _ in neigh_sum:
        pass
    links.drain()


def local(features, tile_vals, tile_cols, row_counts, degrees, w_self, w_neigh, cotangent):
    f_in, f_out = w_self.shape
    _, _, row_tiles, slots = tile_cols.shape
    col_tiles = lax.axis_size(("section", "dp")) * ROWS // TILE
    nodes = lax.axis_size(("section", "replica", "dp")) * ROWS
    slot = jnp.arange(slots, dtype=jnp.int32)
    live = slot[None, :] < row_counts[0, 0][:, None]
    hit = live[:, None, :] & (tile_cols[0, 0][:, None, :] == jnp.arange(col_tiles, dtype=jnp.int32)[None, :, None])
    slot_of = jnp.min(jnp.where(hit, slot[None, None, :], slots), axis=-1)

    def vmem(*shape, dtype=BF16):
        return pltpu.VMEM(shape, dtype)

    def sum_buffers():
        depth = f_in // 2
        return [
            vmem(f_in, f_out), vmem(depth, f_out), vmem(depth, f_out), vmem(NX - 1, depth // NX, f_out),
            vmem(depth // NX, f_out, dtype=F32), vmem(NX * NX - 1, 8, 128, dtype=F32),
            vmem(depth // NX, f_out, dtype=F32), vmem(f_in, f_out),
        ]

    scratch = [vmem(slots + 1, TILE, TILE) for _ in range(row_tiles)] + [
        vmem(row_tiles * TILE, col_tiles * TILE),
        vmem(col_tiles * TILE, f_out),
        vmem(row_tiles * TILE, f_out, dtype=F32),
        vmem(ROWS, f_out, dtype=F32),
        vmem(f_in, ROWS),
        vmem(NX - 1, ROWS, f_out),
        vmem(NX - 1, ROWS, f_out),
        vmem(f_out, NX * ROWS),
        vmem(NX, NX, f_out, ROWS),
        vmem(NX, NX, f_out, ROWS),
        vmem(NX, NX, f_out, ROWS),
        vmem(2, NX, QUARTER, ROWS),
        vmem(2, NX, HALF, ROWS),
        vmem(2, NX, QUARTER, ROWS),
        vmem(2, NX, HALF, ROWS),
        vmem(NX, HALF, ROWS),
        vmem(NX, HALF, ROWS),
        vmem(2, QUARTER, ROWS),
        vmem(2, HALF, ROWS),
        vmem(2, QUARTER, ROWS),
        vmem(2, HALF, ROWS),
        vmem(ROWS, f_in, dtype=F32),
        *sum_buffers(),
        *sum_buffers(),
        pltpu.SemaphoreType.DMA((row_tiles,)),
        pltpu.SemaphoreType.DMA((N_SEND,)),
        pltpu.SemaphoreType.DMA((N_SEND,)),
    ]
    in_vmem = pl.BlockSpec(memory_space=pltpu.VMEM)
    hidden, grad_features, grad_self, grad_neigh = pl.pallas_call(
        functools.partial(kernel, 1.0 / math.sqrt(nodes)),
        out_shape=(
            jax.ShapeDtypeStruct((ROWS, f_out), BF16),
            jax.ShapeDtypeStruct((ROWS, f_in), BF16),
            jax.ShapeDtypeStruct((f_in, f_out), F32),
            jax.ShapeDtypeStruct((f_in, f_out), F32),
        ),
        in_specs=[
            in_vmem,
            pl.BlockSpec(memory_space=pl.ANY),
            pl.BlockSpec(memory_space=pltpu.SMEM),
            in_vmem, in_vmem, in_vmem, in_vmem,
        ],
        out_specs=(in_vmem,) * 4,
        scratch_shapes=scratch,
        compiler_params=pltpu.CompilerParams(
            collective_id=0, has_side_effects=True, vmem_limit_bytes=58 * 1024 * 1024
        ),
        name="sage_layer",
    )(
        features[0],
        tile_vals.reshape(row_tiles * slots, TILE, TILE),
        slot_of,
        degrees,
        w_self,
        w_neigh,
        cotangent[0],
    )
    return hidden[None], grad_features[None], grad_self, grad_neigh


def solution(mesh):
    node = P(("section", "dp"), "replica", None)
    placed = (
        node,
        P(("section", "dp"), "replica", None, None, None, None),
        P(("section", "dp"), "replica", None, None),
        P(("section", "dp"), "replica", None),
        P(("section", "dp"), "replica"),
        P(),
        P(),
        node,
    )
    return jax.shard_map(local, mesh=mesh, in_specs=placed, out_specs=(node, node, P(), P()), check_vma=False)
```

time: 399 us -> 114 us (0.29)
  waiting for transfers between devices: 280 us -> 0 us
  Pallas kernels: 0 us -> 104 us
  matrix products: 65 us -> 0 us
  local copies, waits for them, and re-layouts: 25.4 us -> 6.97 us
  between operations: 13.9 us -> 0.64 us
  other arithmetic: 12.8 us -> 2.19 us
    psum x1 -> x0, waiting for transfers between devices: 139 us -> none  [local(): lax.psum((self_local, neigh_local), ('section', 'replica', 'dp'))]
    reduce_scatter x2 -> x0, waiting for transfers between devices: 111 us -> none  [the longest x1 90 us: local(): lax.psum_scatter(back_terms.astype(jnp.bfloat16), ('section', 'dp'), scat...]
    pallas_call x0 -> x1, Pallas kernels: none -> 104 us  [local(): pl.pallas_call(functools.partial(kernel, 1.0 / math.sqrt(nodes)), out_sha...]
    dot_general x9 -> x0, matrix products: 65 us -> none  [the longest x1 24.6 us: spread_rows(): jnp.einsum('iak,kf->iaf', bands, col_rows, preferred_element_type=jnp.flo...]
    all_gather x2 -> x0, waiting for transfers between devices: 28.8 us -> none  [the longest x1 28.8 us: local(): gathered = lax.all_gather(own_rows, ('section', 'dp'), axis=0, tiled=True)]
    reshape x1 -> x0, local copies, waits for them, and re-layouts: 23.4 us -> none  [build_bands(): bands.astype(jnp.bfloat16)]
    mul x2 -> x0, other arithmetic: 12 us -> none  [the longest x1 10.7 us: local(): tile_vals[0, 0] * slot_live[:, :, None, None].astype(tile_vals.dtype)]
    unnamed x18 -> x4, local copies, waits for them, and re-layouts: 2.03 us -> 6.97 us
  transfers between devices with their start and end apart: 5 -> 0, of which waited for: 4 -> 0; matrix products, arithmetic and copies ran while one was open for 19% -> 0% of each run, Pallas kernels for 0% -> 0%
where the time goes in v1:
time: 114 us
  Pallas kernels  104 us (91%)
  local copies, waits for them, and re-layouts  6.97 us (6%)
  other arithmetic  2.19 us (2%)
    pallas_call x1, Pallas kernels, local(): pl.pallas_call(functools.partial(kernel, 1.0 / math.sqrt(nodes)), out_sha...  104 us
    unnamed x4, local copies, waits for them, and re-layouts  6.97 us

profile of v1, /device:TPU:1, one launch (start us, length us, event | category | flops | bytes accessed | tf_op | source)
XLA Modules:
  0.0 114.2 jit_solution(9825314222404371929)
XLA Ops:
  0.6 0.7 iota_compare_fusion.1
  1.4 1.5 %select_reduce_fusion.slot_ref = s32[8,64]{1,0:T(8,128)} fusion(s32[8,48]{1,0:T(8,128)} %bitcast.12, pred[8,48]{1,0:T(8,128)(4,1)S(1)} %iota_compare_fusion.1), kind=kLoop, calls=%fused_computation | loop fusion | flops 97792 | bytes 3968 | tf_op jit(solution)/shard_map/reduce_min | solution.py:416
  2.8 104.4 %sage_layer.1 = (bf16[256,256]{1,0:T(8,128)(2,1)}, bf16[256,512]{1,0:T(8,128)(2,1)}, f32[512,256]{1,0:T(8,128)}, f32[512,256]{1,0:T(8,128)}) custom-call(bf16[256,512]{1,0:T(8,128)(2,1)} %bitcast.8, bf16[384,128,128]{2,1,0:T(8,128)(2,1)} %bitcast.7, s32[8,64]{1,0:T(8,128)} %select_reduce_fusion.slot_ref, s32[1,256]{1,0:T(1,128)} %deg_ref.1, ...), custom_call_target="tpu_custom_call" | custom-call | tf_op jit(solution)/shard_map/sage_layer/pallas_call | solution.py:459
  107.2 1.6 %copy.16 = bf16[1,256,256]{2,1,0:T(8,128)(2,1)} copy(bf16[1,256,256]{2,1,0:T(8,128)(2,1)} %bitcast.11) | data formatting | bytes 262144
  108.8 1.7 %copy.17 = bf16[1,256,512]{2,1,0:T(8,128)(2,1)} copy(bf16[1,256,512]{2,1,0:T(8,128)(2,1)} %bitcast.9) | data formatting | bytes 524288
  110.4 1.9 %copy.18 = f32[512,256]{1,0:T(8,128)} copy(f32[512,256]{1,0:T(8,128)} %get-tuple-element.18) | data formatting | bytes 1048576
  112.3 1.9 %copy.19 = f32[512,256]{1,0:T(8,128)} copy(f32[512,256]{1,0:T(8,128)} %get-tuple-element.19) | data formatting | bytes 1048576

commit v2 on v1

v2 whole, which is shorter than its diff:
```python
import functools
import math

import jax
import jax.numpy as jnp
from jax import lax
from jax.experimental import pallas as pl
from jax.experimental.pallas import tpu as pltpu
from jax.sharding import PartitionSpec as P

MESH = pl.DeviceIdType.MESH
BF16 = jnp.bfloat16
F32 = jnp.float32
NX = 4
TILE = 128
ROWS = 256
HALF = 128
QUARTER = 64
STRIP = NX * ROWS
N_SEND = 224


def dot(a, b):
    return jnp.dot(a, b, preferred_element_type=F32)


def dot_nt(a, b):
    return lax.dot_general(a, b, (((1,), (1,)), ((), ())), preferred_element_type=F32)


class Links:
    def __init__(self, send_sem, recv_sem):
        self.send_sem, self.recv_sem, self.count, self.sent = send_sem, recv_sem, 0, []

    def send(self, src, dst, device):
        copy = pltpu.make_async_remote_copy(
            src_ref=src,
            dst_ref=dst,
            send_sem=self.send_sem.at[self.count],
            recv_sem=self.recv_sem.at[self.count],
            device_id=device,
            device_id_type=MESH,
        )
        self.count += 1
        copy.start()
        self.sent.append(copy)
        return copy

    def drain(self):
        for copy in self.sent:
            copy.wait_send()


def kernel(
    x_ref, tiles_hbm, cols_ref, counts_ref, deg_ref, ws_ref, wn_ref, cot_ref,
    hid_ref, gf_ref, gs_ref, gn_ref,
    *scratch,
):
    row_tiles, slots = cols_ref.shape
    tile_refs, scratch = scratch[:row_tiles], scratch[row_tiles:]
    (
        table, slot_ref, bands, y_all, acc, self_pre, rdeg, part_out, part_in, ht, pair_out, pair_in, sums,
        az_s, az_b, bx_s, bx_b, mid_a, mid_b, ax, bz, x_row, x_col, own_gf,
        *rest,
    ) = scratch
    self_bufs, neigh_bufs, (tile_sem, table_sem, send_sem, recv_sem) = rest[:6], rest[6:12], rest[12:]

    section = lax.axis_index("section")
    x, core = section // 2, section % 2
    y, z = lax.axis_index("replica"), lax.axis_index("dp")
    links = Links(send_sem, recv_sem)

    def place(px, pc, py, pz):
        return {"section": px * 2 + pc, "replica": py, "dp": pz}

    def at(dx=0, dy=0, dz=0, flip=False):
        return place(lax.rem(x + dx, NX), 1 - core if flip else core, lax.rem(y + dy, NX), lax.rem(z + dz, NX))

    barrier = pltpu.get_barrier_semaphore()
    peers = [at(flip=True)] + [at(dx=d) for d in (1, 3, 2)] + [at(dz=d) for d in (1, 3, 2)] + [at(dy=d) for d in (1, 3, 2)]
    for peer in peers:
        pl.semaphore_signal(barrier, inc=1, device_id=peer, device_id_type=MESH)

    tile_copies = []
    for i in range(row_tiles):
        copy = pltpu.make_async_copy(
            tiles_hbm.at[pl.ds(i * slots, slots)], tile_refs[i].at[pl.ds(0, slots)], tile_sem.at[i]
        )
        copy.start()
        tile_copies.append(copy)

    own = x_ref[...]
    me = (x * 2 + core) * NX + z
    y_all[pl.ds(pl.multiple_of(me * ROWS, ROWS), ROWS), :] = dot(own, wn_ref[...]).astype(BF16)
    pl.semaphore_wait(barrier, len(peers))

    def block(du, dv, h=None, quarter=None):
        dx, dz = (dv, du) if h == 1 else (du, dv)
        start = ((lax.rem(x + dx, NX) * 2 + core) * NX + lax.rem(z + dz, NX)) * ROWS
        size = ROWS
        if h is not None:
            start, size = start + h * HALF, HALF
        if quarter is not None:
            start, size = start + quarter * QUARTER, QUARTER
        return y_all.at[pl.ds(pl.multiple_of(start, QUARTER), size), :]

    def along(h, d):
        return at(dx=d) if h == 0 else at(dz=d)

    def push(h, d, du, dv, quarter=None):
        ref = block(du, dv, h, quarter)
        return links.send(ref, ref, along(1 - h, d))

    def to_partner(dx, dz):
        ref = block(dx, dz)
        partner[dx, dz] = links.send(ref, ref, at(flip=True))

    def make_rows(i):
        tile_copies[i].wait()

        def put(q, carry):
            for k in range(8):
                c = q * 8 + k
                bands[pl.ds(i * TILE, TILE), pl.ds(pl.multiple_of(c * TILE, TILE), TILE)] = tile_refs[i][slot_ref[i, c]]
            return carry

        lax.fori_loop(0, bands.shape[1] // TILE // 8, put, 0)

    partner, line, far, relay = {}, {}, {}, {}
    for d in (1, 3, 2):
        for h in (0, 1):
            line[h, NX - d] = links.send(block(0, 0), block(0, 0), along(h, d))
    to_partner(0, 0)

    shape = cols_ref.shape
    row_id = lax.broadcasted_iota(jnp.int32, shape, 0)
    count = jnp.zeros(shape, jnp.int32)
    for i in range(row_tiles):
        count = jnp.where(row_id == i, counts_ref[i], count)
    live = jnp.where(lax.broadcasted_iota(jnp.int32, shape, 1) < count, cols_ref[...], -1)
    col_id = lax.broadcasted_iota(jnp.int32, table.shape, 1)
    found = jnp.full(table.shape, slots, jnp.int32)
    for m in range(slots):
        found = jnp.where(live[:, m : m + 1] == col_id, m, found)
    table[...] = found
    table_copy = pltpu.make_async_copy(table, slot_ref, table_sem)
    table_copy.start()
    for i in range(row_tiles):
        tile_refs[i][slots] = jnp.zeros((TILE, TILE), BF16)
    table_copy.wait()
    for i in range(0, 4):
        make_rows(i)

    for du in (3, 1):
        for h in (0, 1):
            line[h, du].wait_recv()
            far[h, du, 3] = push(h, 1, du, 0)
            far[h, du, 1] = push(h, 3, du, 0)
            to_partner(*((du, 0) if h == 0 else (0, du)))
    self_pre[...] = dot(own, ws_ref[...])
    for i in range(4, 6):
        make_rows(i)
    for h in (0, 1):
        line[h, 2].wait_recv()
        far[h, 2, 3] = push(h, 1, 2, 0)
        far[h, 2, 1] = push(h, 3, 2, 0)
        far[h, 2, 2] = push(h, 2, 2, 0)
        to_partner(*((2, 0) if h == 0 else (0, 2)))
    for i in range(6, 8):
        make_rows(i)

    def strip_of(dx, flip):
        c = 1 - core if flip else core
        return pl.ds(pl.multiple_of((lax.rem(x + dx, NX) * 2 + c) * STRIP, STRIP), STRIP)

    def spread(dx, flip, first=False):
        if flip:
            for dz in range(NX):
                partner[dx, dz].wait_recv()
        cols = strip_of(dx, flip)
        value = dot(bands[:, cols], y_all[cols, :])
        acc[...] = value if first else acc[...] + value

    for du in (3, 1):
        for dv in (3, 1):
            for h in (0, 1):
                far[h, du, dv].wait_recv()
                relay[h, du, dv] = push(h, 1 if dv == 3 else 3, du, dv, 0 if dv == 3 else 1)
    for dx in (3, 1):
        for dz in (3, 1):
            to_partner(dx, dz)
    spread(0, False, True)
    for h in (0, 1):
        for dv in (3, 1, 2):
            far[h, 2, dv].wait_recv()
    to_partner(2, 2)
    for du in (3, 1):
        for h in (0, 1):
            relay[h, du, 3].wait_recv()
            relay[h, du, 1].wait_recv()
        to_partner(du, 2)
        to_partner(2, du)
    x_row[0] = own
    x_col[0] = own
    x_lines = []
    for d in (2, 1, 3):
        x_lines.append(links.send(x_ref, x_row.at[NX - d], at(dx=d)))
        x_lines.append(links.send(x_ref, x_col.at[NX - d], at(dz=d)))
    spread(0, True)
    spread(3, False)
    spread(1, False)
    spread(3, True)
    spread(1, True)
    rdeg[...] = 1.0 / jnp.broadcast_to(deg_ref[...].astype(F32), (ROWS, ROWS)).T
    for dz in range(NX):
        partner[2, dz].wait_recv()
    own_cols, flip_cols = strip_of(2, False), strip_of(2, True)

    def last_rows(dy):
        rows = pl.ds(pl.multiple_of(lax.rem(y + dy, NX) * ROWS, ROWS), ROWS)
        return acc[rows, :] + dot(bands[rows, own_cols], y_all[own_cols, :]) + dot(bands[rows, flip_cols], y_all[flip_cols, :])

    parts = []
    for d in (2, 1, 3):
        part_out[d - 1] = last_rows(d).astype(BF16)
        parts.append(links.send(part_out.at[d - 1], part_in.at[d - 1], at(dy=d)))
    total = last_rows(0)
    for part in parts:
        part.wait_recv()
    total = total + part_in[0].astype(F32) + part_in[1].astype(F32) + part_in[2].astype(F32)

    preact = self_pre[...] + total * rdeg[...]
    sig = jax.nn.sigmoid(preact)
    grad_pre = (cot_ref[...].astype(F32) * (sig * (1.0 + preact * (1.0 - sig)))).astype(BF16)
    own_rows = pl.ds(pl.multiple_of(y * ROWS, ROWS), ROWS)
    ht[:, own_rows] = (grad_pre.astype(F32) * rdeg[...]).T.astype(BF16)
    grads = [links.send(ht.at[:, own_rows], ht.at[:, own_rows], at(dy=d)) for d in (2, 1, 3)]
    hid_ref[...] = (preact * sig).astype(BF16)
    own_gf[...] = dot_nt(grad_pre, ws_ref[...])

    z_one, z_two = z + 1 - 2 * (z % 2), NX - 1 - z
    half_bit = lax.rem((z + 1) // 2, 2)

    def all_sum(value, out_ref, bufs):
        a_out, a_in, b_out, b_in, c_in, result = bufs
        depth = a_in.shape[0]
        seg = depth // 8
        mine = pl.ds(pl.multiple_of(core * depth, depth), depth)
        other = pl.ds(pl.multiple_of((1 - core) * depth, depth), depth)
        a_out[...] = value.astype(BF16)
        copy = links.send(a_out.at[other, :], a_in, at(flip=True))
        yield
        copy.wait_recv()
        b_out[...] = (a_out[mine, :].astype(F32) + a_in[...].astype(F32)).astype(BF16)

        def seg_at(d, flip_z, base=0):
            bit = 1 - half_bit if flip_z else half_bit
            return pl.ds(pl.multiple_of(base + (lax.rem(y + d, NX) * 2 + bit) * seg, seg), seg)

        group = [(2, True), (2, False), (1, True), (3, True), (1, False), (3, False), (0, True)]

        def first_peer(d, flip_z):
            return place(x, core, lax.rem(y + d, NX), z_one if flip_z else z)

        copies = [
            links.send(b_out.at[seg_at(*to), :], b_in.at[n], first_peer(*to)) for n, to in enumerate(group)
        ]
        yield
        piece = b_out[seg_at(0, False), :].astype(F32)
        for n, copy in enumerate(copies):
            copy.wait_recv()
            piece = piece + b_in[n].astype(F32)
        slot = x * 2 + z // 2
        c_in[slot] = piece.astype(BF16)
        copies = [
            links.send(c_in.at[slot], c_in.at[slot], place(lax.rem(x + d, NX), core, y, z_two if flip_z else z))
            for d, flip_z in group
        ]
        yield
        for copy in copies:
            copy.wait_recv()
        piece = c_in[0].astype(F32)
        for n in range(1, 8):
            piece = piece + c_in[n].astype(F32)
        rows = seg_at(0, False, core * depth)
        result[rows, :] = piece.astype(BF16)
        copies = [links.send(result.at[rows, :], result.at[rows, :], first_peer(*to)) for to in group]
        yield
        for copy in copies:
            copy.wait_recv()
        copy = links.send(result.at[mine, :], result.at[mine, :], at(flip=True))
        yield
        copy.wait_recv()
        out_ref[...] = result[...]
        yield

    self_sum = all_sum(dot(grad_pre.astype(F32).T.astype(BF16), own), gs_ref, self_bufs)
    next(self_sum)
    for copy in grads:
        copy.wait_recv()

    def collect(dx, flip):
        return dot(ht[...], bands[:, strip_of(dx, flip)])

    def add(a, b):
        return (a.astype(F32) + b.astype(F32)).astype(BF16)

    def add3(a, b, c):
        return a.astype(F32) + b.astype(F32) + c.astype(F32)

    pair, a1, a2, b1, b2, fold = {}, {}, {}, {}, {}, []
    lo, hi, half_a, half_b = pl.ds(0, QUARTER), pl.ds(QUARTER, QUARTER), pl.ds(0, HALF), pl.ds(HALF, HALF)
    b_lo, b_hi = pl.ds(HALF, QUARTER), pl.ds(HALF + QUARTER, QUARTER)

    def z_at(d):
        return lax.rem(z + d, NX)

    def give(dx):
        value = collect(dx, True).astype(BF16)
        for k in range(NX):
            pair_out[dx, k] = value[:, k * ROWS : (k + 1) * ROWS]
        pair[dx] = links.send(pair_out.at[dx], pair_in.at[dx], at(flip=True))

    def keep(dx):
        value = collect(dx, False)
        pair[dx].wait_recv()
        for k in range(NX):
            sums[dx, k] = (value[:, k * ROWS : (k + 1) * ROWS] + pair_in[dx, k].astype(F32)).astype(BF16)
        a1[dx] = (
            links.send(sums.at[dx, z_at(2), lo], az_s.at[0, dx], at(dz=1)),
            links.send(sums.at[dx, z_at(2), hi], az_s.at[1, dx], at(dz=3)),
        )

    def a_relay(dx):
        up, down = a1[dx]
        up.wait_recv()
        sums[dx, z_at(1), lo] = add(sums[dx, z_at(1), lo], az_s[0, dx])
        first = links.send(sums.at[dx, z_at(1), half_a], az_b.at[0, dx], at(dz=1))
        down.wait_recv()
        sums[dx, z_at(3), hi] = add(sums[dx, z_at(3), hi], az_s[1, dx])
        second = links.send(sums.at[dx, z_at(3), half_a], az_b.at[1, dx], at(dz=3))
        a2[dx] = (first, second)

    def a_close(dx):
        for copy in a2[dx]:
            copy.wait_recv()
        mid_a[dx] = add3(sums[dx, z, half_a], az_b[0, dx], az_b[1, dx]).astype(BF16)
        if dx:
            fold.append(links.send(mid_a.at[dx], ax.at[dx - 1], at(dx=dx)))

    def b_open():
        for dz in (2, 1, 3, 0):
            b1[dz] = (
                links.send(sums.at[2, z_at(dz), b_lo], bx_s.at[0, dz], at(dx=1)),
                links.send(sums.at[2, z_at(dz), b_hi], bx_s.at[1, dz], at(dx=3)),
            )

    def b_relay(side):
        dx, part = (1, b_lo) if side == 0 else (3, b_hi)
        for dz in (2, 1, 3, 0):
            b1[dz][side].wait_recv()
            sums[dx, z_at(dz), part] = add(sums[dx, z_at(dz), part], bx_s[side, dz])
            b2[side, dz] = links.send(sums.at[dx, z_at(dz), half_b], bx_b.at[side, dz], at(dx=dx))

    def b_close(dz):
        b2[0, dz].wait_recv()
        b2[1, dz].wait_recv()
        mid_b[dz] = add3(sums[0, z_at(dz), half_b], bx_b[0, dz], bx_b[1, dz]).astype(BF16)
        if dz:
            fold.append(links.send(mid_b.at[dz], bz.at[dz - 1], at(dz=dz)))

    give(2)
    give(1)
    keep(2)
    b_open()
    next(self_sum)
    give(3)
    keep(1)
    a_relay(2)
    b_relay(0)
    give(0)
    keep(3)
    a_relay(1)
    b_relay(1)
    keep(0)
    next(self_sum)
    a_relay(3)
    a_relay(0)
    for d in (2, 1):
        a_close(d)
        b_close(d)
    next(self_sum)
    for d in (3, 0):
        a_close(d)
        b_close(d)

    for copy in x_lines:
        copy.wait_recv()
    top, bottom = dot(mid_a[0], x_row[0]), dot(mid_b[0], x_col[0])
    for d in range(1, NX):
        top, bottom = top + dot(mid_a[d], x_row[d]), bottom + dot(mid_b[d], x_col[d])
    neigh_sum = all_sum(jnp.concatenate([top, bottom], axis=0), gn_ref, neigh_bufs)
    next(neigh_sum)
    next(self_sum)
    next(neigh_sum)
    for copy in fold:
        copy.wait_recv()
    sum_a = mid_a[0].astype(F32) + add3(ax[0], ax[1], ax[2])
    sum_b = mid_b[0].astype(F32) + add3(bz[0], bz[1], bz[2])
    back = jnp.concatenate([sum_a, sum_b], axis=0).T.astype(BF16)
    gf_ref[...] = (own_gf[...] + dot_nt(back, wn_ref[...])).astype(BF16)
    for _ in self_sum:
        pass
    for _ in neigh_sum:
        pass
    links.drain()


def finish(node_scale, hid_in, gf_in, gs_in, gn_in, hid_ref, gf_ref, gs_ref, gn_ref):
    hid_ref[...] = hid_in[...]
    gf_ref[...] = gf_in[...]
    gs_ref[...] = gs_in[...].astype(F32).T * node_scale
    gn_ref[...] = gn_in[...].astype(F32).T * node_scale


def local(features, tile_vals, tile_cols, row_counts, degrees, w_self, w_neigh, cotangent):
    f_in, f_out = w_self.shape
    _, _, row_tiles, slots = tile_cols.shape
    col_tiles = lax.axis_size(("section", "dp")) * ROWS // TILE
    nodes = lax.axis_size(("section", "replica", "dp")) * ROWS

    def vmem(*shape, dtype=BF16):
        return pltpu.VMEM(shape, dtype)

    def sum_buffers():
        depth = f_out // 2
        return [
            vmem(f_out, f_in), vmem(depth, f_in), vmem(depth, f_in), vmem(7, depth // 8, f_in),
            vmem(8, depth // 8, f_in), vmem(f_out, f_in),
        ]

    scratch = [vmem(slots + 1, TILE, TILE) for _ in range(row_tiles)] + [
        vmem(row_tiles, 128, dtype=jnp.int32),
        pltpu.SMEM((row_tiles, 128), jnp.int32),
        vmem(row_tiles * TILE, col_tiles * TILE),
        vmem(col_tiles * TILE, f_out),
        vmem(row_tiles * TILE, f_out, dtype=F32),
        vmem(ROWS, f_out, dtype=F32),
        vmem(ROWS, ROWS, dtype=F32),
        vmem(NX - 1, ROWS, f_out),
        vmem(NX - 1, ROWS, f_out),
        vmem(f_out, NX * ROWS),
        vmem(NX, NX, f_out, ROWS),
        vmem(NX, NX, f_out, ROWS),
        vmem(NX, NX, f_out, ROWS),
        vmem(2, NX, QUARTER, ROWS),
        vmem(2, NX, HALF, ROWS),
        vmem(2, NX, QUARTER, ROWS),
        vmem(2, NX, HALF, ROWS),
        vmem(NX, HALF, ROWS),
        vmem(NX, HALF, ROWS),
        vmem(NX - 1, HALF, ROWS),
        vmem(NX - 1, HALF, ROWS),
        vmem(NX, ROWS, f_in),
        vmem(NX, ROWS, f_in),
        vmem(ROWS, f_in, dtype=F32),
        *sum_buffers(),
        *sum_buffers(),
        pltpu.SemaphoreType.DMA((row_tiles,)),
        pltpu.SemaphoreType.DMA,
        pltpu.SemaphoreType.DMA((N_SEND,)),
        pltpu.SemaphoreType.DMA((N_SEND,)),
    ]
    in_vmem = pl.BlockSpec(memory_space=pltpu.VMEM)
    in_smem = pl.BlockSpec(memory_space=pltpu.SMEM)
    raw = pl.pallas_call(
        kernel,
        out_shape=(
            jax.ShapeDtypeStruct((ROWS, f_out), BF16),
            jax.ShapeDtypeStruct((ROWS, f_in), BF16),
            jax.ShapeDtypeStruct((f_out, f_in), BF16),
            jax.ShapeDtypeStruct((f_out, f_in), BF16),
        ),
        in_specs=[in_vmem, pl.BlockSpec(memory_space=pl.ANY), in_vmem, in_smem, in_vmem, in_vmem, in_vmem, in_vmem],
        out_specs=(in_vmem,) * 4,
        scratch_shapes=scratch,
        compiler_params=pltpu.CompilerParams(
            collective_id=0, has_side_effects=True, vmem_limit_bytes=58 * 1024 * 1024
        ),
        name="sage_layer",
    )(
        features[0],
        tile_vals.reshape(row_tiles * slots, TILE, TILE),
        tile_cols[0, 0],
        row_counts[0, 0],
        degrees,
        w_self,
        w_neigh,
        cotangent[0],
    )
    hidden, grad_features, grad_self, grad_neigh = pl.pallas_call(
        functools.partial(finish, 1.0 / math.sqrt(nodes)),
        out_shape=(
            jax.ShapeDtypeStruct((ROWS, f_out), BF16),
            jax.ShapeDtypeStruct((ROWS, f_in), BF16),
            jax.ShapeDtypeStruct((f_in, f_out), F32),
            jax.ShapeDtypeStruct((f_in, f_out), F32),
        ),
        in_specs=[in_vmem] * 4,
        out_specs=(in_vmem,) * 4,
        name="finish",
    )(*raw)
    return hidden[None], grad_features[None], grad_self, grad_neigh


def solution(mesh):
    node = P(("section", "dp"), "replica", None)
    placed = (
        node,
        P(("section", "dp"), "replica", None, None, None, None),
        P(("section", "dp"), "replica", None, None),
        P(("section", "dp"), "replica", None),
        P(("section", "dp"), "replica"),
        P(),
        P(),
        node,
    )
    return jax.shard_map(local, mesh=mesh, in_specs=placed, out_specs=(node, node, P(), P()), check_vma=False)
```

time: 114 us -> 96.4 us (0.85)
  Pallas kernels: 104 us -> 95.6 us
  local copies, waits for them, and re-layouts: 6.97 us -> 0 us
  other arithmetic: 2.19 us -> 0 us
    pallas_call x1 -> x2, Pallas kernels: 104 us -> 95.6 us  [the longest x1 93.2 us: local(): pl.pallas_call(kernel, out_shape=(jax.ShapeDtypeStruct((ROWS, f_out), BF1...]
    unnamed x4 -> x0, local copies, waits for them, and re-layouts: 6.97 us -> none
    reduce_min x1 -> x0, other arithmetic: 1.46 us -> none  [local(): slot_of = jnp.min(jnp.where(hit, slot[None, None, :], slots), axis=-1)]
where the time goes in v2:
time: 96.4 us; the launch traced here: 96.2 us
  Pallas kernels  95.6 us (99%)
    pallas_call x1, Pallas kernels, local(): pl.pallas_call(kernel, out_shape=(jax.ShapeDtypeStruct((ROWS, f_out), BF1...  93.2 us
    pallas_call x1, Pallas kernels, local(): pl.pallas_call(functools.partial(finish, 1.0 / math.sqrt(nodes)), out_sha...  2.43 us

profile of v2, /device:TPU:1, one launch (start us, length us, event | category | flops | bytes accessed | tf_op | source)
XLA Modules:
  0.0 96.2 jit_solution(14336319344670911187)
XLA Ops:
  0.6 93.2 %sage_layer.1 = (bf16[256,256]{1,0:T(8,128)(2,1)}, bf16[256,512]{1,0:T(8,128)(2,1)}, bf16[256,512]{1,0:T(8,128)(2,1)}, bf16[256,512]{1,0:T(8,128)(2,1)}) custom-call(bf16[256,512]{1,0:T(8,128)(2,1)} %bitcast.8, bf16[384,128,128]{2,1,0:T(8,128)(2,1)} %bitcast.7, s32[8,48]{1,0:T(8,128)} %bitcast.10, s32[8]{0:T(128)} %bitcast.11, s32[1,256]{1,0:T(1,128)} %deg_ref.1, ...), custom_call_target="tpu_custom_call" | custom-call | tf_op jit(solution)/shard_map/sage_layer/pallas_call | solution.py:476
  93.8 2.4 %finish.1 = (bf16[256,256]{1,0:T(8,128)(2,1)}, bf16[256,512]{1,0:T(8,128)(2,1)}, f32[512,256]{1,0:T(8,128)}, f32[512,256]{1,0:T(8,128)}) custom-call(bf16[256,256]{1,0:T(8,128)(2,1)} %get-tuple-element.12.hid_in, bf16[256,512]{1,0:T(8,128)(2,1)} %get-tuple-element.13.gf_in, bf16[256,512]{1,0:T(8,128)(2,1)} %get-tuple-element.14.gs_in, ...), custom_call_target="tpu_custom_call" | custom-call | tf_op jit(solution)/shard_map/finish/pallas_call | solution.py:501

commit v3 on v2

v3 whole, which is shorter than its diff:
```python
import functools
import math

import jax
import jax.numpy as jnp
from jax import lax
from jax.experimental import pallas as pl
from jax.experimental.pallas import tpu as pltpu
from jax.sharding import PartitionSpec as P

MESH = pl.DeviceIdType.MESH
BF16 = jnp.bfloat16
F32 = jnp.float32
NX = 4
TILE = 128
ROWS = 256
HALF = 128
QUARTER = 64
STRIP = NX * ROWS
N_SEND = 24
N_RECV = 64


def dot(a, b):
    return jnp.dot(a, b, preferred_element_type=F32)


def dot_nt(a, b):
    return lax.dot_general(a, b, (((1,), (1,)), ((), ())), preferred_element_type=F32)


class Links:
    def __init__(self, send_sem, recv_sem):
        self.send_sem, self.recv_sem = send_sem, recv_sem
        self.groups, self.sent = 0, []

    def group(self):
        self.groups += 1
        return self.recv_sem.at[self.groups - 1]

    def send(self, src, dst, device, group=None):
        count = len(self.sent)
        if count >= N_SEND:
            self.sent[count - N_SEND].wait_send()
        copy = pltpu.make_async_remote_copy(
            src_ref=src,
            dst_ref=dst,
            send_sem=self.send_sem.at[count % N_SEND],
            recv_sem=self.group() if group is None else group,
            device_id=device,
            device_id_type=MESH,
        )
        copy.start()
        self.sent.append(copy)
        return copy

    def drain(self):
        for copy in self.sent[-N_SEND:]:
            copy.wait_send()


def wait_all(group, view):
    pltpu.make_async_copy(view, view, group).wait()


def kernel(
    x_hbm, tiles_hbm, cols_hbm, counts_ref, deg_hbm, ws_hbm, wn_hbm, cot_hbm,
    hid_hbm, gf_hbm, gs_hbm, gn_hbm,
    *scratch,
):
    row_tiles, slots = cols_hbm.shape
    tile_refs, scratch = scratch[:row_tiles], scratch[row_tiles:]
    (
        table, slot_ref, bands, y_all, acc, self_pre, rdeg, part_out, part_in, ht, pair_out, pair_in, sums,
        az, bx, mid_a, mid_b, ax, bz, x_row, x_col, own_gf,
        x_ref, cols_ref, deg_ref, ws_ref, wn_ref, cot_ref, hid_ref, gf_ref, gs_ref, gn_ref,
        *rest,
    ) = scratch
    self_bufs, neigh_bufs, (tile_sem, io_sem, send_sem, recv_sem) = rest[:6], rest[6:12], rest[12:]

    io_copies = []

    def io_copy(src, dst):
        copy = pltpu.make_async_copy(src, dst, io_sem.at[len(io_copies)])
        io_copies.append(copy)
        copy.start()
        return copy

    x_in, wn_in = io_copy(x_hbm, x_ref), io_copy(wn_hbm, wn_ref)

    section = lax.axis_index("section")
    x, core = section // 2, section % 2
    y, z = lax.axis_index("replica"), lax.axis_index("dp")
    links = Links(send_sem, recv_sem)

    def place(px, pc, py, pz):
        return {"section": px * 2 + pc, "replica": py, "dp": pz}

    def at(dx=0, dy=0, dz=0, flip=False):
        return place(lax.rem(x + dx, NX), 1 - core if flip else core, lax.rem(y + dy, NX), lax.rem(z + dz, NX))

    barrier = pltpu.get_barrier_semaphore()
    peers = [at(flip=True)] + [at(dx=d) for d in (1, 3, 2)] + [at(dz=d) for d in (1, 3, 2)] + [at(dy=d) for d in (1, 3, 2)]
    for peer in peers:
        pl.semaphore_signal(barrier, inc=1, device_id=peer, device_id_type=MESH)

    tile_copies = []
    for i in range(row_tiles):
        copy = pltpu.make_async_copy(
            tiles_hbm.at[pl.ds(i * slots, slots)], tile_refs[i].at[pl.ds(0, slots)], tile_sem.at[i]
        )
        copy.start()
        tile_copies.append(copy)

    cols_in, ws_in, deg_in, cot_in = (
        io_copy(cols_hbm, cols_ref), io_copy(ws_hbm, ws_ref), io_copy(deg_hbm, deg_ref), io_copy(cot_hbm, cot_ref)
    )
    x_in.wait()
    wn_in.wait()
    own = x_ref[...]
    me = (x * 2 + core) * NX + z
    y_all[pl.ds(pl.multiple_of(me * ROWS, ROWS), ROWS), :] = dot(own, wn_ref[...]).astype(BF16)
    pl.semaphore_wait(barrier, len(peers))

    def block(du, dv, h=None, quarter=None):
        dx, dz = (dv, du) if h == 1 else (du, dv)
        start = ((lax.rem(x + dx, NX) * 2 + core) * NX + lax.rem(z + dz, NX)) * ROWS
        size = ROWS
        if h is not None:
            start, size = start + h * HALF, HALF
        if quarter is not None:
            start, size = start + quarter * QUARTER, QUARTER
        return y_all.at[pl.ds(pl.multiple_of(start, QUARTER), size), :]

    def along(h, d):
        return at(dx=d) if h == 0 else at(dz=d)

    def push(h, d, du, dv, quarter=None, group=None):
        ref = block(du, dv, h, quarter)
        return links.send(ref, ref, along(1 - h, d), group)

    partner = [links.group() for _ in range(NX)]

    def to_partner(dx, dz):
        ref = block(dx, dz)
        links.send(ref, ref, at(flip=True), partner[dx])

    def make_rows(i):
        tile_copies[i].wait()

        def put(q, carry):
            for k in range(8):
                c = q * 8 + k
                bands[pl.ds(i * TILE, TILE), pl.ds(pl.multiple_of(c * TILE, TILE), TILE)] = tile_refs[i][slot_ref[i, c]]
            return carry

        lax.fori_loop(0, bands.shape[1] // TILE // 8, put, 0)

    line, far = {}, {}
    rest, far_two, relay = ([links.group() for _ in range(n)] for n in (2, 2, 4))
    def send_line(h, d, part, group=None):
        ref = block(0, 0, part)
        line[h, NX - d, part] = links.send(ref, ref, along(h, d), group)

    for d in (1, 3, 2):
        for h in (0, 1):
            send_line(h, d, h)
    to_partner(0, 0)
    for d in (1, 3):
        for h in (0, 1):
            send_line(h, d, 1 - h, rest[h])

    cols_in.wait()
    shape = cols_ref.shape
    row_id = lax.broadcasted_iota(jnp.int32, shape, 0)
    count = jnp.zeros(shape, jnp.int32)
    for i in range(row_tiles):
        count = jnp.where(row_id == i, counts_ref[i], count)
    live = jnp.where(lax.broadcasted_iota(jnp.int32, shape, 1) < count, cols_ref[...], -1)
    col_id = lax.broadcasted_iota(jnp.int32, table.shape, 1)
    found = jnp.full(table.shape, slots, jnp.int32)
    for m in range(slots):
        found = jnp.where(live[:, m : m + 1] == col_id, m, found)
    table[...] = found
    table_copy = io_copy(table, slot_ref)
    for i in range(row_tiles):
        tile_refs[i][slots] = jnp.zeros((TILE, TILE), BF16)
    table_copy.wait()
    for i in range(0, 2):
        make_rows(i)

    for du in (3, 1):
        for h in (0, 1):
            line[h, du, h].wait_recv()
            far[h, du, 3] = push(h, 1, du, 0)
            far[h, du, 1] = push(h, 3, du, 0)
    for h in (0, 1):
        send_line(h, 2, 1 - h)
    ws_in.wait()
    self_pre[...] = dot(own, ws_ref[...])
    for i in range(2, 4):
        make_rows(i)
    for h in (0, 1):
        line[h, 2, h].wait_recv()
        for d in (1, 3, 2):
            push(h, d, 2, 0, group=far_two[h])
    for h in (0, 1):
        wait_all(rest[h], y_all.at[pl.ds(0, 2 * HALF), :])
        for du in (3, 1):
            to_partner(*((du, 0) if h == 0 else (0, du)))
    for i in range(4, 6):
        make_rows(i)

    def strip_of(dx, flip):
        c = 1 - core if flip else core
        return pl.ds(pl.multiple_of((lax.rem(x + dx, NX) * 2 + c) * STRIP, STRIP), STRIP)

    def spread(dx, flip, first=False):
        cols = strip_of(dx, flip)
        if flip:
            wait_all(partner[dx], y_all.at[cols, :])
        value = dot(bands[:, cols], y_all[cols, :])
        acc[...] = value if first else acc[...] + value

    for du in (3, 1):
        for dv in (3, 1):
            for h in (0, 1):
                far[h, du, dv].wait_recv()
                push(h, 1 if dv == 3 else 3, du, dv, 0 if dv == 3 else 1, relay[h + du - 1])
    for dx in (3, 1):
        for dz in (3, 1):
            to_partner(dx, dz)
    for h in (0, 1):
        line[h, 2, 1 - h].wait_recv()
        to_partner(*((2, 0) if h == 0 else (0, 2)))
    for i in range(6, 8):
        make_rows(i)
    spread(0, False, True)
    for h in (0, 1):
        wait_all(far_two[h], y_all.at[pl.ds(0, 3 * HALF), :])
    to_partner(2, 2)
    for du in (3, 1):
        for h in (0, 1):
            wait_all(relay[h + du - 1], block(du, 2, h))
        to_partner(du, 2)
        to_partner(2, du)
    spread(0, True)
    spread(3, False)
    spread(1, False)
    spread(3, True)
    spread(1, True)
    deg_in.wait()
    cot_in.wait()
    rdeg[...] = 1.0 / jnp.broadcast_to(deg_ref[...].astype(F32), (ROWS, ROWS)).T
    own_cols, flip_cols = strip_of(2, False), strip_of(2, True)
    wait_all(partner[2], y_all.at[flip_cols, :])

    def last_rows(dy):
        rows = pl.ds(pl.multiple_of(lax.rem(y + dy, NX) * ROWS, ROWS), ROWS)
        return acc[rows, :] + dot(bands[rows, own_cols], y_all[own_cols, :]) + dot(bands[rows, flip_cols], y_all[flip_cols, :])

    parts = links.group()
    for d in (2, 1, 3):
        part_out[d - 1] = last_rows(d).astype(BF16)
        links.send(part_out.at[d - 1], part_in.at[d - 1], at(dy=d), parts)
    x_row[0] = own
    x_col[0] = own
    row_in, col_in = links.group(), links.group()
    for d in (2, 1, 3):
        links.send(x_ref, x_row.at[NX - d], at(dx=d), row_in)
        links.send(x_ref, x_col.at[NX - d], at(dz=d), col_in)
    total = last_rows(0)
    wait_all(parts, part_in)
    total = total + part_in[0].astype(F32) + part_in[1].astype(F32) + part_in[2].astype(F32)

    preact = self_pre[...] + total * rdeg[...]
    sig = jax.nn.sigmoid(preact)
    grad_pre = (cot_ref[...].astype(F32) * (sig * (1.0 + preact * (1.0 - sig)))).astype(BF16)
    own_rows = pl.ds(pl.multiple_of(y * ROWS, ROWS), ROWS)
    ht[:, own_rows] = (grad_pre.astype(F32) * rdeg[...]).T.astype(BF16)
    grads = links.group()
    for d in (2, 1, 3):
        links.send(ht.at[:, own_rows], ht.at[:, own_rows], at(dy=d), grads)
    hid_ref[...] = (preact * sig).astype(BF16)
    hid_out = io_copy(hid_ref, hid_hbm)
    own_gf[...] = dot_nt(grad_pre, ws_ref[...])

    z_one, z_two = z + 1 - 2 * (z % 2), NX - 1 - z
    half_bit = lax.rem((z + 1) // 2, 2)

    def all_sum(value, out_ref, bufs):
        a_out, a_in, b_out, b_in, c_in, result = bufs
        depth = a_in.shape[0]
        seg = depth // 8
        mine = pl.ds(pl.multiple_of(core * depth, depth), depth)
        other = pl.ds(pl.multiple_of((1 - core) * depth, depth), depth)
        a_out[...] = value.astype(BF16)
        copy = links.send(a_out.at[other, :], a_in, at(flip=True))
        yield
        copy.wait_recv()
        b_out[...] = (a_out[mine, :].astype(F32) + a_in[...].astype(F32)).astype(BF16)

        def seg_at(d, flip_z, base=0):
            bit = 1 - half_bit if flip_z else half_bit
            return pl.ds(pl.multiple_of(base + (lax.rem(y + d, NX) * 2 + bit) * seg, seg), seg)

        group = [(2, True), (2, False), (1, True), (3, True), (1, False), (3, False), (0, True)]

        def first_peer(d, flip_z):
            return place(x, core, lax.rem(y + d, NX), z_one if flip_z else z)

        arrived = links.group()
        for n, to in enumerate(group):
            links.send(b_out.at[seg_at(*to), :], b_in.at[n], first_peer(*to), arrived)
        yield
        wait_all(arrived, b_in)
        piece = b_out[seg_at(0, False), :].astype(F32)
        for n in range(7):
            piece = piece + b_in[n].astype(F32)
        slot = x * 2 + z // 2
        c_in[slot] = piece.astype(BF16)
        arrived = links.group()
        for d, flip_z in group:
            peer = place(lax.rem(x + d, NX), core, y, z_two if flip_z else z)
            links.send(c_in.at[slot], c_in.at[slot], peer, arrived)
        yield
        wait_all(arrived, c_in.at[pl.ds(0, 7)])
        piece = c_in[0].astype(F32)
        for n in range(1, 8):
            piece = piece + c_in[n].astype(F32)
        rows = seg_at(0, False, core * depth)
        result[rows, :] = piece.astype(BF16)
        arrived = links.group()
        for to in group:
            links.send(result.at[rows, :], result.at[rows, :], first_peer(*to), arrived)
        yield
        wait_all(arrived, result.at[pl.ds(0, 7 * seg), :])
        copy = links.send(result.at[mine, :], result.at[mine, :], at(flip=True))
        yield
        copy.wait_recv()
        out_ref[...] = result[...]
        yield

    self_sum = all_sum(dot(grad_pre.astype(F32).T.astype(BF16), own), gs_ref, self_bufs)
    next(self_sum)
    next(self_sum)
    wait_all(grads, ht.at[:, pl.ds(0, (NX - 1) * ROWS)])

    def collect(dx, flip):
        return dot(ht[...], bands[:, strip_of(dx, flip)])

    def add3(a, b, c):
        return a.astype(F32) + b.astype(F32) + c.astype(F32)

    pair, a_lines = {}, [links.group() for _ in range(NX)]
    b_lines, a_fold, b_fold = links.group(), links.group(), links.group()
    half_a, half_b = pl.ds(0, HALF), pl.ds(HALF, HALF)

    def z_at(d):
        return lax.rem(z + d, NX)

    def give(dx):
        value = collect(dx, True).astype(BF16)
        for k in range(NX):
            pair_out[dx, k] = value[:, k * ROWS : (k + 1) * ROWS]
        pair[dx] = links.send(pair_out.at[dx], pair_in.at[dx], at(flip=True))

    def keep(dx):
        value = collect(dx, False)
        pair[dx].wait_recv()
        for k in range(NX):
            sums[dx, k] = (value[:, k * ROWS : (k + 1) * ROWS] + pair_in[dx, k].astype(F32)).astype(BF16)
        for d in (2, 1, 3):
            links.send(sums.at[dx, z_at(d), half_a], az.at[dx, d - 1], at(dz=d), a_lines[dx])
        if dx:
            links.send(sums.at[dx, :, half_b], bx.at[dx - 1], at(dx=dx), b_lines)

    def a_close(dx):
        wait_all(a_lines[dx], az.at[dx])
        total = sums[dx, z, half_a].astype(F32) + add3(az[dx, 0], az[dx, 1], az[dx, 2])
        mid_a[dx] = total.astype(BF16)
        if dx:
            links.send(mid_a.at[dx], ax.at[dx - 1], at(dx=dx), a_fold)

    def b_close(dz):
        total = sums[0, z_at(dz), half_b].astype(F32) + add3(bx[0, z_at(dz)], bx[1, z_at(dz)], bx[2, z_at(dz)])
        mid_b[dz] = total.astype(BF16)
        if dz:
            links.send(mid_b.at[dz], bz.at[dz - 1], at(dz=dz), b_fold)

    give(2)
    give(1)
    keep(2)
    give(3)
    keep(1)
    give(0)
    keep(3)
    keep(0)
    next(self_sum)
    a_close(2)
    a_close(1)
    a_close(3)
    wait_all(b_lines, bx)
    for d in (2, 1, 3, 0):
        b_close(d)
    a_close(0)

    wait_all(row_in, x_row.at[pl.ds(1, NX - 1)])
    wait_all(col_in, x_col.at[pl.ds(1, NX - 1)])
    top, bottom = dot(mid_a[0], x_row[0]), dot(mid_b[0], x_col[0])
    for d in range(1, NX):
        top, bottom = top + dot(mid_a[d], x_row[d]), bottom + dot(mid_b[d], x_col[d])
    neigh_sum = all_sum(jnp.concatenate([top, bottom], axis=0), gn_ref, neigh_bufs)
    next(neigh_sum)
    next(self_sum)
    next(neigh_sum)
    next(self_sum)
    wait_all(a_fold, ax)
    wait_all(b_fold, bz)
    sum_a = mid_a[0].astype(F32) + add3(ax[0], ax[1], ax[2])
    sum_b = mid_b[0].astype(F32) + add3(bz[0], bz[1], bz[2])
    back = jnp.concatenate([sum_a, sum_b], axis=0).T.astype(BF16)
    gf_ref[...] = (own_gf[...] + dot_nt(back, wn_ref[...])).astype(BF16)
    gf_out = io_copy(gf_ref, gf_hbm)
    for _ in self_sum:
        pass
    gs_out = io_copy(gs_ref, gs_hbm)
    for _ in neigh_sum:
        pass
    gn_out = io_copy(gn_ref, gn_hbm)
    links.drain()
    for copy in (hid_out, gf_out, gs_out, gn_out):
        copy.wait()


def finish(node_scale, hid_in, gf_in, gs_in, gn_in, hid_ref, gf_ref, gs_ref, gn_ref):
    hid_ref[...] = hid_in[...]
    gf_ref[...] = gf_in[...]
    gs_ref[...] = gs_in[...].astype(F32).T * node_scale
    gn_ref[...] = gn_in[...].astype(F32).T * node_scale


def local(features, tile_vals, tile_cols, row_counts, degrees, w_self, w_neigh, cotangent):
    f_in, f_out = w_self.shape
    _, _, row_tiles, slots = tile_cols.shape
    col_tiles = lax.axis_size(("section", "dp")) * ROWS // TILE
    nodes = lax.axis_size(("section", "replica", "dp")) * ROWS

    def vmem(*shape, dtype=BF16):
        return pltpu.VMEM(shape, dtype)

    def sum_buffers():
        depth = f_out // 2
        return [
            vmem(f_out, f_in), vmem(depth, f_in), vmem(depth, f_in), vmem(7, depth // 8, f_in),
            vmem(8, depth // 8, f_in), vmem(f_out, f_in),
        ]

    scratch = [vmem(slots + 1, TILE, TILE) for _ in range(row_tiles)] + [
        vmem(row_tiles, 128, dtype=jnp.int32),
        pltpu.SMEM((row_tiles, 128), jnp.int32),
        vmem(row_tiles * TILE, col_tiles * TILE),
        vmem(col_tiles * TILE, f_out),
        vmem(row_tiles * TILE, f_out, dtype=F32),
        vmem(ROWS, f_out, dtype=F32),
        vmem(ROWS, ROWS, dtype=F32),
        vmem(NX - 1, ROWS, f_out),
        vmem(NX - 1, ROWS, f_out),
        vmem(f_out, NX * ROWS),
        vmem(NX, NX, f_out, ROWS),
        vmem(NX, NX, f_out, ROWS),
        vmem(NX, NX, f_out, ROWS),
        vmem(NX, NX - 1, HALF, ROWS),
        vmem(NX - 1, NX, HALF, ROWS),
        vmem(NX, HALF, ROWS),
        vmem(NX, HALF, ROWS),
        vmem(NX - 1, HALF, ROWS),
        vmem(NX - 1, HALF, ROWS),
        vmem(NX, ROWS, f_in),
        vmem(NX, ROWS, f_in),
        vmem(ROWS, f_in, dtype=F32),
        vmem(ROWS, f_in),
        vmem(row_tiles, slots, dtype=jnp.int32),
        vmem(1, ROWS, dtype=jnp.int32),
        vmem(f_in, f_out),
        vmem(f_in, f_out),
        vmem(ROWS, f_out),
        vmem(ROWS, f_out),
        vmem(ROWS, f_in),
        vmem(f_out, f_in),
        vmem(f_out, f_in),
        *sum_buffers(),
        *sum_buffers(),
        pltpu.SemaphoreType.DMA((row_tiles,)),
        pltpu.SemaphoreType.DMA((16,)),
        pltpu.SemaphoreType.DMA((N_SEND,)),
        pltpu.SemaphoreType.DMA((N_RECV,)),
    ]
    in_vmem = pl.BlockSpec(memory_space=pltpu.VMEM)
    in_smem = pl.BlockSpec(memory_space=pltpu.SMEM)
    in_any = pl.BlockSpec(memory_space=pl.ANY)
    raw = pl.pallas_call(
        kernel,
        out_shape=(
            jax.ShapeDtypeStruct((ROWS, f_out), BF16),
            jax.ShapeDtypeStruct((ROWS, f_in), BF16),
            jax.ShapeDtypeStruct((f_out, f_in), BF16),
            jax.ShapeDtypeStruct((f_out, f_in), BF16),
        ),
        in_specs=[in_any, in_any, in_any, in_smem, in_any, in_any, in_any, in_any],
        out_specs=(in_any,) * 4,
        scratch_shapes=scratch,
        compiler_params=pltpu.CompilerParams(
            collective_id=0, has_side_effects=True, vmem_limit_bytes=58 * 1024 * 1024
        ),
        name="sage_layer",
    )(
        features[0],
        tile_vals.reshape(row_tiles * slots, TILE, TILE),
        tile_cols[0, 0],
        row_counts[0, 0],
        degrees,
        w_self,
        w_neigh,
        cotangent[0],
    )
    hidden, grad_features, grad_self, grad_neigh = pl.pallas_call(
        functools.partial(finish, 1.0 / math.sqrt(nodes)),
        out_shape=(
            jax.ShapeDtypeStruct((ROWS, f_out), BF16),
            jax.ShapeDtypeStruct((ROWS, f_in), BF16),
            jax.ShapeDtypeStruct((f_in, f_out), F32),
            jax.ShapeDtypeStruct((f_in, f_out), F32),
        ),
        in_specs=[in_vmem] * 4,
        out_specs=(in_vmem,) * 4,
        name="finish",
    )(*raw)
    return hidden[None], grad_features[None], grad_self, grad_neigh


def solution(mesh):
    node = P(("section", "dp"), "replica", None)
    placed = (
        node,
        P(("section", "dp"), "replica", None, None, None, None),
        P(("section", "dp"), "replica", None, None),
        P(("section", "dp"), "replica", None),
        P(("section", "dp"), "replica"),
        P(),
        P(),
        node,
    )
    return jax.shard_map(local, mesh=mesh, in_specs=placed, out_specs=(node, node, P(), P()), check_vma=False)
```

time: 96.4 us -> 86.7 us (0.90)
  Pallas kernels: 95.6 us -> 85.9 us
    pallas_call x1, Pallas kernels: 93.2 us -> 83.5 us  [local(): pl.pallas_call(kernel, out_shape=(jax.ShapeDtypeStruct((ROWS, f_out), BF1...]
where the time goes in v3:
time: 86.7 us; the launch traced here: 86.5 us
  Pallas kernels  85.9 us (99%)
    pallas_call x1, Pallas kernels, local(): pl.pallas_call(kernel, out_shape=(jax.ShapeDtypeStruct((ROWS, f_out), BF1...  83.5 us
    pallas_call x1, Pallas kernels, local(): pl.pallas_call(functools.partial(finish, 1.0 / math.sqrt(nodes)), out_sha...  2.43 us

profile of v3, /device:TPU:1, one launch (start us, length us, event | category | flops | bytes accessed | tf_op | source)
XLA Modules:
  0.0 86.5 jit_solution(13673691419133753762)
XLA Ops:
  0.6 83.5 %sage_layer.1 = (bf16[256,256]{1,0:T(8,128)(2,1)}, bf16[256,512]{1,0:T(8,128)(2,1)}, bf16[256,512]{1,0:T(8,128)(2,1)}, bf16[256,512]{1,0:T(8,128)(2,1)}) custom-call(bf16[256,512]{1,0:T(8,128)(2,1)} %bitcast.8, bf16[384,128,128]{2,1,0:T(8,128)(2,1)} %bitcast.7, s32[8,48]{1,0:T(8,128)} %bitcast.10, s32[8]{0:T(128)} %bitcast.11, s32[1,256]{1,0:T(1,128)} %deg_hbm.1, ...), custom_call_target="tpu_custom_call" | custom-call | tf_op jit(solution)/shard_map/sage_layer/pallas_call | solution.py:502
  84.1 2.4 %finish.1 = (bf16[256,256]{1,0:T(8,128)(2,1)}, bf16[256,512]{1,0:T(8,128)(2,1)}, f32[512,256]{1,0:T(8,128)}, f32[512,256]{1,0:T(8,128)}) custom-call(bf16[256,256]{1,0:T(8,128)(2,1)} %get-tuple-element.12.hid_in, bf16[256,512]{1,0:T(8,128)(2,1)} %get-tuple-element.13.gf_in, bf16[256,512]{1,0:T(8,128)(2,1)} %get-tuple-element.14.gs_in, ...), custom_call_target="tpu_custom_call" | custom-call | tf_op jit(solution)/shard_map/finish/pallas_call | solution.py:527

commit v4 on v3

--- a/solution.py
+++ b/solution.py
@@ -18,7 +18,7 @@
 QUARTER = 64
 STRIP = NX * ROWS
 N_SEND = 24
-N_RECV = 64
+N_RECV = 66
 
 
 def dot(a, b):
@@ -36,6 +36,7 @@
 
     def group(self):
         self.groups += 1
+        assert self.groups <= N_RECV
         return self.recv_sem.at[self.groups - 1]
 
     def send(self, src, dst, device, group=None):
@@ -72,8 +73,8 @@
     tile_refs, scratch = scratch[:row_tiles], scratch[row_tiles:]
     (
         table, slot_ref, bands, y_all, acc, self_pre, rdeg, part_out, part_in, ht, pair_out, pair_in, sums,
-        az, bx, mid_a, mid_b, ax, bz, x_row, x_col, own_gf,
-        x_ref, cols_ref, deg_ref, ws_ref, wn_ref, cot_ref, hid_ref, gf_ref, gs_ref, gn_ref,
+        az, bx, mid_a, mid_b, ax, bz, x_all, own_gf,
+        cols_ref, deg_ref, ws_ref, wn_ref, cot_ref, hid_ref, gf_ref, gs_ref, gn_ref,
         *rest,
     ) = scratch
     self_bufs, neigh_bufs, (tile_sem, io_sem, send_sem, recv_sem) = rest[:6], rest[6:12], rest[12:]
@@ -86,12 +87,23 @@
         copy.start()
         return copy
 
-    x_in, wn_in = io_copy(x_hbm, x_ref), io_copy(wn_hbm, wn_ref)
 
     section = lax.axis_index("section")
     x, core = section // 2, section % 2
     y, z = lax.axis_index("replica"), lax.axis_index("dp")
     links = Links(send_sem, recv_sem)
+
+    def x_block(dx, dz, h=None, quarter=None):
+        start = (lax.rem(x + dx, NX) * NX + lax.rem(z + dz, NX)) * ROWS
+        size = ROWS
+        if h is not None:
+            start, size = start + h * HALF, HALF
+        if quarter is not None:
+            start, size = start + quarter * QUARTER, QUARTER
+        return x_all.at[pl.ds(pl.multiple_of(start, QUARTER), size), :]
+
+    x_own = x_block(0, 0)
+    x_in, wn_in = io_copy(x_hbm, x_own), io_copy(wn_hbm, wn_ref)
 
     def place(px, pc, py, pz):
         return {"section": px * 2 + pc, "replica": py, "dp": pz}
@@ -117,7 +129,7 @@
     )
     x_in.wait()
     wn_in.wait()
-    own = x_ref[...]
+    own = x_own[...]
     me = (x * 2 + core) * NX + z
     y_all[pl.ds(pl.multiple_of(me * ROWS, ROWS), ROWS), :] = dot(own, wn_ref[...]).astype(BF16)
     pl.semaphore_wait(barrier, len(peers))
@@ -244,6 +256,21 @@
             wait_all(relay[h + du - 1], block(du, 2, h))
         to_partner(du, 2)
         to_partner(2, du)
+    x_line, x_far = {}, {}
+    x_late = links.group()
+
+    def x_push(h, d, du, dv=0, quarter=None, group=None):
+        ref = x_block(*((du, dv) if h == 0 else (dv, du)), h, quarter)
+        return links.send(ref, ref, along(1 - h, d), group)
+
+    for d in (1, 3, 2):
+        for h in (0, 1):
+            ref = x_block(0, 0, h)
+            x_line[h, NX - d] = links.send(ref, ref, along(h, d))
+    for d in (1, 3, 2):
+        for h in (0, 1):
+            ref = x_block(0, 0, 1 - h)
+            links.send(ref, ref, along(h, d), x_late)
     spread(0, True)
     spread(3, False)
     spread(1, False)
@@ -263,12 +290,15 @@
     for d in (2, 1, 3):
         part_out[d - 1] = last_rows(d).astype(BF16)
         links.send(part_out.at[d - 1], part_in.at[d - 1], at(dy=d), parts)
-    x_row[0] = own
-    x_col[0] = own
-    row_in, col_in = links.group(), links.group()
-    for d in (2, 1, 3):
-        links.send(x_ref, x_row.at[NX - d], at(dx=d), row_in)
-        links.send(x_ref, x_col.at[NX - d], at(dz=d), col_in)
+    for du in (3, 1):
+        for h in (0, 1):
+            x_line[h, du].wait_recv()
+            for d in (1, 3):
+                x_far[h, du, NX - d] = x_push(h, d, du)
+    for h in (0, 1):
+        x_line[h, 2].wait_recv()
+        for d in (1, 3, 2):
+            x_push(h, d, 2, group=x_late)
     total = last_rows(0)
     wait_all(parts, part_in)
     total = total + part_in[0].astype(F32) + part_in[1].astype(F32) + part_in[2].astype(F32)
@@ -344,6 +374,11 @@
     self_sum = all_sum(dot(grad_pre.astype(F32).T.astype(BF16), own), gs_ref, self_bufs)
     next(self_sum)
     next(self_sum)
+    for du in (3, 1):
+        for dv in (3, 1):
+            for h in (0, 1):
+                x_far[h, du, dv].wait_recv()
+                x_push(h, 1 if dv == 3 else 3, du, dv, 0 if dv == 3 else 1, x_late)
     wait_all(grads, ht.at[:, pl.ds(0, (NX - 1) * ROWS)])
 
     def collect(dx, flip):
@@ -396,7 +431,19 @@
     give(0)
     keep(3)
     keep(0)
+
+    wait_all(x_late, x_all.at[pl.ds(0, 12 * HALF + 8 * QUARTER), :])
+
+    def x_strip(dx):
+        return x_all[pl.ds(pl.multiple_of(lax.rem(x + dx, NX) * STRIP, STRIP), STRIP), :]
+
+    term = dot(jnp.concatenate([sums[0, k] for k in range(NX)], axis=1), x_strip(0))
+    for dx in range(1, NX):
+        term = term + dot(jnp.concatenate([sums[dx, k] for k in range(NX)], axis=1), x_strip(dx))
+    neigh_sum = all_sum(term, gn_ref, neigh_bufs)
+    next(neigh_sum)
     next(self_sum)
+    next(neigh_sum)
     a_close(2)
     a_close(1)
     a_close(3)
@@ -404,17 +451,8 @@
     for d in (2, 1, 3, 0):
         b_close(d)
     a_close(0)
-
-    wait_all(row_in, x_row.at[pl.ds(1, NX - 1)])
-    wait_all(col_in, x_col.at[pl.ds(1, NX - 1)])
-    top, bottom = dot(mid_a[0], x_row[0]), dot(mid_b[0], x_col[0])
-    for d in range(1, NX):
-        top, bottom = top + dot(mid_a[d], x_row[d]), bottom + dot(mid_b[d], x_col[d])
-    neigh_sum = all_sum(jnp.concatenate([top, bottom], axis=0), gn_ref, neigh_bufs)
-    next(neigh_sum)
     next(self_sum)
     next(neigh_sum)
-    next(self_sum)
     wait_all(a_fold, ax)
     wait_all(b_fold, bz)
     sum_a = mid_a[0].astype(F32) + add3(ax[0], ax[1], ax[2])
@@ -476,10 +514,8 @@
         vmem(NX, HALF, ROWS),
         vmem(NX - 1, HALF, ROWS),
         vmem(NX - 1, HALF, ROWS),
-        vmem(NX, ROWS, f_in),
-        vmem(NX, ROWS, f_in),
+        vmem(NX * STRIP, f_in),
         vmem(ROWS, f_in, dtype=F32),
-        vmem(ROWS, f_in),
         vmem(row_tiles, slots, dtype=jnp.int32),
         vmem(1, ROWS, dtype=jnp.int32),
         vmem(f_in, f_out),

time: 86.7 us -> 82.2 us (0.948)
  Pallas kernels: 85.9 us -> 81.4 us
    pallas_call x1, Pallas kernels: 83.5 us -> 79 us  [local(): pl.pallas_call(kernel, out_shape=(jax.ShapeDtypeStruct((ROWS, f_out), BF1...]
where the time goes in v4:
time: 82.2 us; the launch traced here: 82.1 us
  Pallas kernels  81.4 us (99%)
    pallas_call x1, Pallas kernels, local(): pl.pallas_call(kernel, out_shape=(jax.ShapeDtypeStruct((ROWS, f_out), BF1...  79 us
    pallas_call x1, Pallas kernels, local(): pl.pallas_call(functools.partial(finish, 1.0 / math.sqrt(nodes)), out_sha...  2.43 us

profile of v4, /device:TPU:1, one launch (start us, length us, event | category | flops | bytes accessed | tf_op | source)
XLA Modules:
  0.0 82.1 jit_solution(12948331632506525519)
XLA Ops:
  0.6 79.0 %sage_layer.1 = (bf16[256,256]{1,0:T(8,128)(2,1)}, bf16[256,512]{1,0:T(8,128)(2,1)}, bf16[256,512]{1,0:T(8,128)(2,1)}, bf16[256,512]{1,0:T(8,128)(2,1)}) custom-call(bf16[256,512]{1,0:T(8,128)(2,1)} %bitcast.8, bf16[384,128,128]{2,1,0:T(8,128)(2,1)} %bitcast.7, s32[8,48]{1,0:T(8,128)} %bitcast.10, s32[8]{0:T(128)} %bitcast.11, s32[1,256]{1,0:T(1,128)} %deg_hbm.1, ...), custom_call_target="tpu_custom_call" | custom-call | tf_op jit(solution)/shard_map/sage_layer/pallas_call | solution.py:538
  79.7 2.4 %finish.1 = (bf16[256,256]{1,0:T(8,128)(2,1)}, bf16[256,512]{1,0:T(8,128)(2,1)}, f32[512,256]{1,0:T(8,128)}, f32[512,256]{1,0:T(8,128)}) custom-call(bf16[256,256]{1,0:T(8,128)(2,1)} %get-tuple-element.12.hid_in, bf16[256,512]{1,0:T(8,128)(2,1)} %get-tuple-element.13.gf_in, bf16[256,512]{1,0:T(8,128)(2,1)} %get-tuple-element.14.gs_in, ...), custom_call_target="tpu_custom_call" | custom-call | tf_op jit(solution)/shard_map/finish/pallas_call | solution.py:563

commit v5 on v4

--- a/solution.py
+++ b/solution.py
@@ -18,7 +18,7 @@
 QUARTER = 64
 STRIP = NX * ROWS
 N_SEND = 24
-N_RECV = 66
+N_RECV = 74
 
 
 def dot(a, b):
@@ -72,7 +72,7 @@
     row_tiles, slots = cols_hbm.shape
     tile_refs, scratch = scratch[:row_tiles], scratch[row_tiles:]
     (
-        table, slot_ref, bands, y_all, acc, self_pre, rdeg, part_out, part_in, ht, pair_out, pair_in, sums,
+        table, slot_ref, bands, y_all, acc, self_pre, rdeg, part_out, part_in, pre_out, ht, pair_out, pair_in, sums,
         az, bx, mid_a, mid_b, ax, bz, x_all, own_gf,
         cols_ref, deg_ref, ws_ref, wn_ref, cot_ref, hid_ref, gf_ref, gs_ref, gn_ref,
         *rest,
@@ -263,14 +263,26 @@
         ref = x_block(*((du, dv) if h == 0 else (dv, du)), h, quarter)
         return links.send(ref, ref, along(1 - h, d), group)
 
-    for d in (1, 3, 2):
+    x_rest, x_two = ([links.group() for _ in range(2)] for _ in range(2))
+
+    def x_on(h, half, du, group):
+        ref = x_block(*((du, 0) if h == 0 else (0, du)), half, 0 if du == 3 else 1)
+        links.send(ref, ref, along(h, 1 if du == 3 else 3), group)
+
+    def x_relay(du):
+        for dv in (3, 1):
+            for h in (0, 1):
+                x_far[h, du, dv].wait_recv()
+                x_push(h, 1 if dv == 3 else 3, du, dv, 0 if dv == 3 else 1, x_late)
+
+    for d in (1, 3):
         for h in (0, 1):
             ref = x_block(0, 0, h)
             x_line[h, NX - d] = links.send(ref, ref, along(h, d))
-    for d in (1, 3, 2):
+    for d in (1, 3):
         for h in (0, 1):
             ref = x_block(0, 0, 1 - h)
-            links.send(ref, ref, along(h, d), x_late)
+            links.send(ref, ref, along(h, d), x_rest[h])
     spread(0, True)
     spread(3, False)
     spread(1, False)
@@ -278,41 +290,63 @@
     spread(1, True)
     deg_in.wait()
     cot_in.wait()
-    rdeg[...] = 1.0 / jnp.broadcast_to(deg_ref[...].astype(F32), (ROWS, ROWS)).T
+    rdeg[...] = 1.0 / jnp.broadcast_to(deg_ref[...].astype(F32), (HALF, ROWS)).T
     own_cols, flip_cols = strip_of(2, False), strip_of(2, True)
     wait_all(partner[2], y_all.at[flip_cols, :])
+
+    def add3(a, b, c):
+        return a.astype(F32) + b.astype(F32) + c.astype(F32)
 
     def last_rows(dy):
         rows = pl.ds(pl.multiple_of(lax.rem(y + dy, NX) * ROWS, ROWS), ROWS)
         return acc[rows, :] + dot(bands[rows, own_cols], y_all[own_cols, :]) + dot(bands[rows, flip_cols], y_all[flip_cols, :])
 
-    parts = links.group()
+    parts, grads = [links.group() for _ in range(2)], [links.group() for _ in range(2)]
+
+    def send_part(f, d):
+        links.send(part_out.at[f, d - 1], part_in.at[f, d - 1], at(dy=d), parts[f])
+
     for d in (2, 1, 3):
-        part_out[d - 1] = last_rows(d).astype(BF16)
-        links.send(part_out.at[d - 1], part_in.at[d - 1], at(dy=d), parts)
+        value = last_rows(d).astype(BF16)
+        part_out[0, d - 1] = value[:, :HALF]
+        part_out[1, d - 1] = value[:, HALF:]
+        send_part(0, d)
+    for d in (2, 1, 3):
+        send_part(1, d)
     for du in (3, 1):
         for h in (0, 1):
             x_line[h, du].wait_recv()
+            x_on(h, h, du, x_two[h])
+    for du in (3, 1):
+        for h in (0, 1):
             for d in (1, 3):
                 x_far[h, du, NX - d] = x_push(h, d, du)
+    acc[pl.ds(0, ROWS), :] = last_rows(0)
     for h in (0, 1):
-        x_line[h, 2].wait_recv()
-        for d in (1, 3, 2):
-            x_push(h, d, 2, group=x_late)
-    total = last_rows(0)
-    wait_all(parts, part_in)
-    total = total + part_in[0].astype(F32) + part_in[1].astype(F32) + part_in[2].astype(F32)
-
-    preact = self_pre[...] + total * rdeg[...]
-    sig = jax.nn.sigmoid(preact)
-    grad_pre = (cot_ref[...].astype(F32) * (sig * (1.0 + preact * (1.0 - sig)))).astype(BF16)
+        wait_all(x_rest[h], x_all.at[pl.ds(0, 2 * HALF), :])
+        for du in (3, 1):
+            x_on(h, 1 - h, du, x_late)
+    for h in (0, 1):
+        wait_all(x_two[h], x_block(*((2, 0) if h == 0 else (0, 2)), h))
+        for d in (1, 3):
+            x_far[h, 2, NX - d] = x_push(h, d, 2)
+
     own_rows = pl.ds(pl.multiple_of(y * ROWS, ROWS), ROWS)
-    ht[:, own_rows] = (grad_pre.astype(F32) * rdeg[...]).T.astype(BF16)
-    grads = links.group()
-    for d in (2, 1, 3):
-        links.send(ht.at[:, own_rows], ht.at[:, own_rows], at(dy=d), grads)
-    hid_ref[...] = (preact * sig).astype(BF16)
+    for f in range(2):
+        cols = pl.ds(f * HALF, HALF)
+        wait_all(parts[f], part_in.at[f])
+        total = acc[pl.ds(0, ROWS), cols] + add3(part_in[f, 0], part_in[f, 1], part_in[f, 2])
+        preact = self_pre[:, cols] + total * rdeg[...]
+        sig = jax.nn.sigmoid(preact)
+        slope = sig * (1.0 + preact * (1.0 - sig))
+        half_pre = (cot_ref[:, cols].astype(F32) * slope).astype(BF16)
+        ht[cols, own_rows] = (half_pre.astype(F32) * rdeg[...]).T.astype(BF16)
+        for d in (2, 1, 3):
+            links.send(ht.at[cols, own_rows], ht.at[cols, own_rows], at(dy=d), grads[f])
+        pre_out[:, cols] = half_pre
+        hid_ref[:, cols] = (preact * sig).astype(BF16)
     hid_out = io_copy(hid_ref, hid_hbm)
+    grad_pre = pre_out[...]
     own_gf[...] = dot_nt(grad_pre, ws_ref[...])
 
     z_one, z_two = z + 1 - 2 * (z % 2), NX - 1 - z
@@ -374,18 +408,13 @@
     self_sum = all_sum(dot(grad_pre.astype(F32).T.astype(BF16), own), gs_ref, self_bufs)
     next(self_sum)
     next(self_sum)
-    for du in (3, 1):
-        for dv in (3, 1):
-            for h in (0, 1):
-                x_far[h, du, dv].wait_recv()
-                x_push(h, 1 if dv == 3 else 3, du, dv, 0 if dv == 3 else 1, x_late)
-    wait_all(grads, ht.at[:, pl.ds(0, (NX - 1) * ROWS)])
+    x_relay(3)
+    x_relay(1)
+    for f in range(2):
+        wait_all(grads[f], ht.at[pl.ds(f * HALF, HALF), pl.ds(0, (NX - 1) * ROWS)])
 
     def collect(dx, flip):
         return dot(ht[...], bands[:, strip_of(dx, flip)])
-
-    def add3(a, b, c):
-        return a.astype(F32) + b.astype(F32) + c.astype(F32)
 
     pair, a_lines = {}, [links.group() for _ in range(NX)]
     b_lines, a_fold, b_fold = links.group(), links.group(), links.group()
@@ -425,6 +454,7 @@
 
     give(2)
     give(1)
+    x_relay(2)
     keep(2)
     give(3)
     keep(1)
@@ -432,7 +462,7 @@
     keep(3)
     keep(0)
 
-    wait_all(x_late, x_all.at[pl.ds(0, 12 * HALF + 8 * QUARTER), :])
+    wait_all(x_late, x_all.at[pl.ds(0, 16 * QUARTER), :])
 
     def x_strip(dx):
         return x_all[pl.ds(pl.multiple_of(lax.rem(x + dx, NX) * STRIP, STRIP), STRIP), :]
@@ -446,6 +476,7 @@
     next(neigh_sum)
     a_close(2)
     a_close(1)
+    next(neigh_sum)
     a_close(3)
     wait_all(b_lines, bx)
     for d in (2, 1, 3, 0):
@@ -501,9 +532,10 @@
         vmem(col_tiles * TILE, f_out),
         vmem(row_tiles * TILE, f_out, dtype=F32),
         vmem(ROWS, f_out, dtype=F32),
-        vmem(ROWS, ROWS, dtype=F32),
-        vmem(NX - 1, ROWS, f_out),
-        vmem(NX - 1, ROWS, f_out),
+        vmem(ROWS, HALF, dtype=F32),
+        vmem(2, NX - 1, ROWS, HALF),
+        vmem(2, NX - 1, ROWS, HALF),
+        vmem(ROWS, f_out),
         vmem(f_out, NX * ROWS),
         vmem(NX, NX, f_out, ROWS),
         vmem(NX, NX, f_out, ROWS),

time: 82.2 us -> 79.9 us (0.972)
  Pallas kernels: 81.4 us -> 79.2 us
    pallas_call x1, Pallas kernels: 79 us -> 76.7 us  [local(): pl.pallas_call(kernel, out_shape=(jax.ShapeDtypeStruct((ROWS, f_out), BF1...]
where the time goes in v5:
time: 79.9 us; the launch traced here: 79.8 us
  Pallas kernels  79.2 us (99%)
    pallas_call x1, Pallas kernels, local(): pl.pallas_call(kernel, out_shape=(jax.ShapeDtypeStruct((ROWS, f_out), BF1...  76.7 us
    pallas_call x1, Pallas kernels, local(): pl.pallas_call(functools.partial(finish, 1.0 / math.sqrt(nodes)), out_sha...  2.43 us

profile of v5, /device:TPU:1, one launch (start us, length us, event | category | flops | bytes accessed | tf_op | source)
XLA Modules:
  0.0 79.8 jit_solution(6894484421691441957)
XLA Ops:
  0.6 76.7 %sage_layer.1 = (bf16[256,256]{1,0:T(8,128)(2,1)}, bf16[256,512]{1,0:T(8,128)(2,1)}, bf16[256,512]{1,0:T(8,128)(2,1)}, bf16[256,512]{1,0:T(8,128)(2,1)}) custom-call(bf16[256,512]{1,0:T(8,128)(2,1)} %bitcast.8, bf16[384,128,128]{2,1,0:T(8,128)(2,1)} %bitcast.7, s32[8,48]{1,0:T(8,128)} %bitcast.10, s32[8]{0:T(128)} %bitcast.11, s32[1,256]{1,0:T(1,128)} %deg_hbm.1, ...), custom_call_target="tpu_custom_call" | custom-call | tf_op jit(solution)/shard_map/sage_layer/pallas_call | solution.py:570
  77.4 2.4 %finish.1 = (bf16[256,256]{1,0:T(8,128)(2,1)}, bf16[256,512]{1,0:T(8,128)(2,1)}, f32[512,256]{1,0:T(8,128)}, f32[512,256]{1,0:T(8,128)}) custom-call(bf16[256,256]{1,0:T(8,128)(2,1)} %get-tuple-element.12.hid_in, bf16[256,512]{1,0:T(8,128)(2,1)} %get-tuple-element.13.gf_in, bf16[256,512]{1,0:T(8,128)(2,1)} %get-tuple-element.14.gs_in, ...), custom_call_target="tpu_custom_call" | custom-call | tf_op jit(solution)/shard_map/finish/pallas_call | solution.py:595

commit v6 on v5

--- a/solution.py
+++ b/solution.py
@@ -248,6 +248,7 @@
     for i in range(6, 8):
         make_rows(i)
     spread(0, False, True)
+    spread(0, True)
     for h in (0, 1):
         wait_all(far_two[h], y_all.at[pl.ds(0, 3 * HALF), :])
     to_partner(2, 2)
@@ -283,7 +284,6 @@
         for h in (0, 1):
             ref = x_block(0, 0, 1 - h)
             links.send(ref, ref, along(h, d), x_rest[h])
-    spread(0, True)
     spread(3, False)
     spread(1, False)
     spread(3, True)

time: 79.9 us -> 79.3 us (level)
  no operation moved by 1% of the time
where the time goes in v6:
time: 79.3 us; the launch traced here: 79.2 us
  Pallas kernels  78.5 us (99%)
    pallas_call x1, Pallas kernels, local(): pl.pallas_call(kernel, out_shape=(jax.ShapeDtypeStruct((ROWS, f_out), BF1...  76.1 us
    pallas_call x1, Pallas kernels, local(): pl.pallas_call(functools.partial(finish, 1.0 / math.sqrt(nodes)), out_sha...  2.43 us

profile of v6, /device:TPU:1, one launch (start us, length us, event | category | flops | bytes accessed | tf_op | source)
XLA Modules:
  0.0 79.2 jit_solution(6740662635788280291)
XLA Ops:
  0.6 76.1 %sage_layer.1 = (bf16[256,256]{1,0:T(8,128)(2,1)}, bf16[256,512]{1,0:T(8,128)(2,1)}, bf16[256,512]{1,0:T(8,128)(2,1)}, bf16[256,512]{1,0:T(8,128)(2,1)}) custom-call(bf16[256,512]{1,0:T(8,128)(2,1)} %bitcast.8, bf16[384,128,128]{2,1,0:T(8,128)(2,1)} %bitcast.7, s32[8,48]{1,0:T(8,128)} %bitcast.10, s32[8]{0:T(128)} %bitcast.11, s32[1,256]{1,0:T(1,128)} %deg_hbm.1, ...), custom_call_target="tpu_custom_call" | custom-call | tf_op jit(solution)/shard_map/sage_layer/pallas_call | solution.py:570
  76.7 2.4 %finish.1 = (bf16[256,256]{1,0:T(8,128)(2,1)}, bf16[256,512]{1,0:T(8,128)(2,1)}, f32[512,256]{1,0:T(8,128)}, f32[512,256]{1,0:T(8,128)}) custom-call(bf16[256,256]{1,0:T(8,128)(2,1)} %get-tuple-element.12.hid_in, bf16[256,512]{1,0:T(8,128)(2,1)} %get-tuple-element.13.gf_in, bf16[256,512]{1,0:T(8,128)(2,1)} %get-tuple-element.14.gs_in, ...), custom_call_target="tpu_custom_call" | custom-call | tf_op jit(solution)/shard_map/finish/pallas_call | solution.py:595
